TPU v7x, 768 devices: a whole 4x8x12 slice. The times are simulated.
768 devices in a mesh: srv: 384 (over z, y, x), head: 2 (over core).
Axes of the slice: x: 4, y: 8, z: 12, core: 2. Of those that a mesh axis runs over, the one named last changes fastest.
Arguments:
- tokens: bfloat16 [98304, 4096], P(('srv', 'head')), may hold values from -10.5 to 10.5
- doc_ids: int32 [98304], P(('srv', 'head')), may hold values from 0 to 383, never falling along the last dimension, each value on 1 to 512 neighbouring positions
- w_query: bfloat16 [4096, 2048], P(None, 'head'), may hold values from -1 to 1
- w_key: bfloat16 [4096, 512], P(None, 'head'), may hold values from -1.5 to 1.5
- value_weight: bfloat16 [4096, 512], P(None, 'head'), may hold values from -0.09375 to 0.09375
Outputs:
- attended: bfloat16 [98304, 2048], P(('srv', 'head'))
Inputs may be any that keep to these rules, and one draw needn't show every extreme that they name: `doc_ids`: documents are consecutive runs of at most 512 tokens; one has exactly that many.
All inputs are finite; a program needn't handle non-finite values.
Results may differ from a plain program's by a relative error of at most 0.012.
The roundings to bfloat16 on the way count: a program that leaves them out, or rounds other values in their place, can miss the bound.
Values may be sent and summed in bfloat16 or wider, within the bound.
No kernel may reach another device: no remote copies, remote signals or barrier semaphores. Data moves between devices by JAX's collectives and lax.ppermute only.
A program may use at most 64 MiB of HBM per device.

v0:
```python
import jax
import jax.numpy as jnp
from jax import lax
from jax.sharding import PartitionSpec as P

QUERY_HEADS = 16
KEY_VALUE_HEADS = 4
HEAD_SIZE = 128
SPAN = 2


def from_behind(x, axis, by):
    devices = lax.axis_size(axis)
    pairs = [(i, i + by) for i in range(devices) if 0 <= i + by < devices]
    return lax.ppermute(x, axis, pairs)


def on_device(tokens, doc_ids, w_query, w_key, value_weight):
    gathered, group_docs = (
        lax.all_gather(tokens, "head", axis=0, tiled=True),
        lax.all_gather(doc_ids, "head", axis=0, tiled=True),
    )
    group_token = gathered.shape[0]
    local_kv = w_key.shape[1] // HEAD_SIZE
    repeat_factor = QUERY_HEADS // KEY_VALUE_HEADS
    query_row_set = jnp.dot(gathered, w_query, preferred_element_type=jnp.float32).astype(
        jnp.bfloat16
    )
    key_matrix_rows = jnp.dot(gathered, w_key, preferred_element_type=jnp.float32).astype(
        jnp.bfloat16
    )
    value_matrix_rows = jnp.dot(gathered, value_weight, preferred_element_type=jnp.float32).astype(
        jnp.bfloat16
    )
    query_matrix = query_row_set.reshape(group_token, local_kv, repeat_factor, HEAD_SIZE)
    group_index = lax.axis_index("srv")
    query_pos = group_index * group_token + jnp.arange(group_token, dtype=jnp.int32)
    logit_scale = 1.0 / HEAD_SIZE**0.5

    def attend(carried, key_block, value_block, doc_block, distance):
        running, totals, accumulated = carried
        key_pos = (group_index - distance) * group_token + jnp.arange(group_token, dtype=jnp.int32)
        allowed = (
            (group_docs[:, None] == doc_block[None, :])
            & (key_pos[None, :] <= query_pos[:, None])
            & (key_pos[None, :] >= 0)
        )
        score_matrix = (
            jnp.einsum(
                "hfwl,afl->fwha",
                query_matrix,
                key_block.reshape(group_token, local_kv, HEAD_SIZE),
                preferred_element_type=jnp.float32,
            )
            * logit_scale
        )
        score_matrix = jnp.where(allowed[None, None], score_matrix, -1e30)
        newmax = jnp.maximum(running, jnp.max(score_matrix, -1))
        factor = jnp.exp(running - newmax)
        exponent = jnp.exp(score_matrix - newmax[..., None])
        totals = totals * factor + jnp.sum(exponent, -1)
        attention_weight = exponent.astype(jnp.bfloat16)
        accumulated = accumulated * factor[..., None] + jnp.einsum(
            "mjwh,hmn->mjwn",
            attention_weight,
            value_block.reshape(group_token, local_kv, HEAD_SIZE),
            preferred_element_type=jnp.float32,
        )
        return (newmax, totals, accumulated)

    carried = (
        jnp.full((local_kv, repeat_factor, group_token), -1e30, jnp.float32),
        jnp.zeros((local_kv, repeat_factor, group_token), jnp.float32),
        jnp.zeros((local_kv, repeat_factor, group_token, HEAD_SIZE), jnp.float32),
    )
    carried = attend(carried, key_matrix_rows, value_matrix_rows, group_docs, 0)
    for distance in range(1, SPAN + 1):
        key_block, value_block, doc_block = from_behind(
            (key_matrix_rows, value_matrix_rows, group_docs), "srv", distance
        )
        carried = attend(carried, key_block, value_block, doc_block, distance)
    running, totals, accumulated = carried
    result = accumulated / totals[..., None]
    result = (
        jnp.transpose(result, (2, 0, 1, 3))
        .reshape(group_token, local_kv * repeat_factor * HEAD_SIZE)
        .astype(jnp.bfloat16)
    )
    return lax.all_to_all(result, "head", split_axis=0, concat_axis=1, tiled=True)


def solution(mesh):
    in_specs = (
        P(("srv", "head"), None),
        P(("srv", "head")),
        P(None, "head"),
        P(None, "head"),
        P(None, "head"),
    )
    out_specs = P(("srv", "head"), None)
    return jax.shard_map(
        on_device, mesh=mesh, in_specs=in_specs, out_specs=out_specs, check_vma=False
    )
```

profile of v0, /device:TPU:1, one launch (start us, length us, event | category | flops | bytes accessed | tf_op | source)
XLA Modules:
  0.0 89.7 jit_solution(7433394797888983642)
XLA Ops:
  6.5 0.7 all-gather.3.cloned.1.call-update
  7.3 12.1 %all-gather = s32[2,1,128]{2,1,0:T(1,128)S(1)} all-gather(s32[1,1,128]{2,1,0:T(1,128)} %bitcast.138), channel_id=1, replica_groups=mesh['srv'=384,'head'=2] {'head'}, dimensions={0}, use_global_device_ids=true | all-gather | bytes 1536 | tf_op jit(solution)/shard_map/all_gather | solution.py:21
  19.4 1.3 %collective-permute-start.3 = (s32[256]{0:T(256)S(1)}, s32[256]{0:T(256)S(1)}, u32[]{:S(2)}, u32[]{:S(2)}) collective-permute-start(s32[256]{0:T(256)S(1)} %bitcast.135), channel_id=1, source_target_pairs={{0,4},{2,6},{4,8},{6,10},{8,12},{10,14},{12,16},{14,18},{16,20},{1... | collective-permute-start | bytes 3080 | tf_op jit(solution)/shard_map/ppermute | solution.py:15
  20.7 1.3 %collective-permute-start = (s32[256]{0:T(256)S(1)}, s32[256]{0:T(256)S(1)}, u32[]{:S(2)}, u32[]{:S(2)}) collective-permute-start(s32[256]{0:T(256)S(1)} %bitcast.136), channel_id=1, source_target_pairs={{0,2},{2,4},{4,6},{6,8},{8,10},{10,12},{12,14},{14,16},{16,18},{18... | collective-permute-start | bytes 3080 | tf_op jit(solution)/shard_map/ppermute | solution.py:15
  22.1 0.6 collective-permute-done
  22.7 1.1 %and_and_fusion.2 = (pred[256,256]{0,1:T(8,128)(4,1)}, pred[256,256]{0,1:T(8,128)(4,1)S(1)}, pred[256,256]{0,1:T(8,128)(4,1)S(1)}) fusion(s32[256]{0:T(256)S(1)} %iota_add_fusion.2, s32[256]{0:T(256)S(1)} %bitcast.137, pred[256]{0:T(512)(128)(4,1)S(1)} %broadcast_compare_fusion.2, pred[256]{0:T(512)(128)(4,1)S(1)} %broadcast_compare_fusion, ...), kind=kLoop, calls=%fused_computation.43 | loop fusion | flops 786432 | bytes 203520 | tf_op jit(solution)/shard_map/and | solution.py:44
  23.8 17.2 %all-gather.3.cloned.1.call-done = bf16[256,4096]{1,0:T(8,128)(2,1)} async-done(((bf16[128,4096]{1,0:T(8,128)(2,1)}), bf16[256,4096]{1,0:T(8,128)(2,1)}) %all-gather.3.cloned.1.call-update) | async-done | bytes 2097168 | tf_op jit(solution)/shard_map/all_gather | solution.py:20
  41.0 2.7 %convolution_convert_fusion.2 = bf16[256,256]{0,1:T(8,128)(2,1)S(1)} fusion(bf16[256,4096]{1,0:T(8,128)(2,1)} %all-gather.3.cloned.1.call-done, bf16[4096,256]{1,0:T(8,128)(2,1)S(1)} %copy-done), kind=kOutput, calls=%fused_computation.26 | convolution fusion | flops 536936448 | bytes 4325376 | tf_op jit(solution)/shard_map/dot_general | solution.py:29
  43.6 3.5 %collective-permute-start.4 = (bf16[256,256]{0,1:T(8,128)(2,1)S(1)}, bf16[256,256]{0,1:T(8,128)(2,1)}, u32[]{:S(2)}, u32[]{:S(2)}) collective-permute-start(bf16[256,256]{0,1:T(8,128)(2,1)S(1)} %convolution_convert_fusion.2), channel_id=1, source_target_pairs={{0,4},{2,6},{4,8},{6,10},{8,12},{10,14},{12,16},{14,18},{16,20},{1... | collective-permute-start | bytes 393224 | tf_op jit(solution)/shard_map/ppermute | solution.py:15
  47.2 2.8 %collective-permute-start.1 = (bf16[256,256]{0,1:T(8,128)(2,1)S(1)}, bf16[256,256]{0,1:T(8,128)(2,1)}, u32[]{:S(2)}, u32[]{:S(2)}) collective-permute-start(bf16[256,256]{0,1:T(8,128)(2,1)S(1)} %convolution_convert_fusion.2), channel_id=1, source_target_pairs={{0,2},{2,4},{4,6},{6,8},{8,10},{10,12},{12,14},{14,16},{16,18},{18... | collective-permute-start | bytes 393224 | tf_op jit(solution)/shard_map/ppermute | solution.py:15
  50.0 1.0 %convolution_convert_fusion.1 = bf16[256,256]{0,1:T(8,128)(2,1)S(1)} fusion(bf16[256,4096]{1,0:T(8,128)(2,1)S(1)} %copy-done.1, bf16[4096,256]{1,0:T(8,128)(2,1)S(1)} %copy-done.2), kind=kOutput, calls=%fused_computation.25 | convolution fusion | flops 536936448 | bytes 4325376 | tf_op jit(solution)/shard_map/dot_general | solution.py:32
  51.0 4.0 %collective-permute-start.5 = (bf16[256,256]{0,1:T(8,128)(2,1)S(1)}, bf16[256,256]{0,1:T(8,128)(2,1)}, u32[]{:S(2)}, u32[]{:S(2)}) collective-permute-start(bf16[256,256]{0,1:T(8,128)(2,1)S(1)} %convolution_convert_fusion.1), channel_id=1, source_target_pairs={{0,4},{2,6},{4,8},{6,10},{8,12},{10,14},{12,16},{14,18},{16,20},{1... | collective-permute-start | bytes 393224 | tf_op jit(solution)/shard_map/ppermute | solution.py:15
  55.0 3.7 %collective-permute-start.2 = (bf16[256,256]{0,1:T(8,128)(2,1)S(1)}, bf16[256,256]{0,1:T(8,128)(2,1)}, u32[]{:S(2)}, u32[]{:S(2)}) collective-permute-start(bf16[256,256]{0,1:T(8,128)(2,1)S(1)} %convolution_convert_fusion.1), channel_id=1, source_target_pairs={{0,2},{2,4},{4,6},{6,8},{8,10},{10,12},{12,14},{14,16},{16,18},{18... | collective-permute-start | bytes 393224 | tf_op jit(solution)/shard_map/ppermute | solution.py:15
  58.7 5.8 %convolution_convert_fusion = bf16[256,1024]{1,0:T(8,128)(2,1)S(1)} fusion(bf16[256,4096]{1,0:T(8,128)(2,1)S(1)} %copy-done.1, bf16[4096,1024]{1,0:T(8,128)(2,1)} %param.7), kind=kOutput, calls=%fused_computation.23 | convolution fusion | flops 2147745792 | bytes 11010048 | tf_op jit(solution)/shard_map/dot_general | solution.py:26
  64.8 1.4 %fusion.46 = (f32[2,4,256]{2,1,0:T(4,128)S(1)}, f32[2,4,256,256]{2,3,1,0:T(8,128)S(1)}) fusion(bf16[256,2,128,1]{0,2,3,1:T(8,128)(2,1)S(1)} %bitcast.134, bf16[256,2,4,128]{3,2,1,0:T(4,128)(2,1)S(1)} %reshape.313, pred[256,256]{0,1:T(8,128)(4,1)} %get-tuple-element.12), kind=kOutput, calls=%fused_computation.70 | convolution fusion | flops 135788544 | bytes 2826240 | tf_op jit(solution)/shard_map/hfwl,afl->fwha/dot_general | solution.py:49
  66.3 1.5 %fusion.7 = (f32[2,4,256]{2,1,0:T(4,128)S(1)}, f32[2,256,256,4]{2,1,3,0:T(8,128)S(1)}) fusion(pred[256,256]{0,1:T(8,128)(4,1)S(1)} %get-tuple-element.13, bf16[256,2,128,1]{0,2,3,1:T(8,128)(2,1)} %bitcast.37, bf16[256,2,4,128]{3,2,1,0:T(4,128)(2,1)S(1)} %reshape.313), kind=kOutput, calls=%fused_computation.13 | convolution fusion | flops 135788544 | bytes 2826240 | tf_op jit(solution)/shard_map/hfwl,afl->fwha/dot_general | solution.py:49
  67.7 1.5 %fusion.6 = (f32[2,4,256]{2,1,0:T(4,128)S(1)}, f32[2,256,256,4]{2,1,3,0:T(8,128)S(1)}) fusion(pred[256,256]{0,1:T(8,128)(4,1)S(1)} %get-tuple-element.14, bf16[256,2,128,1]{0,2,3,1:T(8,128)(2,1)} %bitcast.33, bf16[256,2,4,128]{3,2,1,0:T(4,128)(2,1)S(1)} %reshape.313), kind=kOutput, calls=%fused_computation.12 | convolution fusion | flops 135788544 | bytes 2826240 | tf_op jit(solution)/shard_map/hfwl,afl->fwha/dot_general | solution.py:49
  69.2 1.6 %convolution_bitcast_fusion = f32[256,2,4,128]{3,0,2,1:T(8,128)S(1)} fusion(bf16[256,2,128,1]{0,2,3,1:T(8,128)(2,1)} %bitcast.39, f32[2,256,256,4]{2,1,3,0:T(8,128)S(1)} %get-tuple-element.16, f32[2,4,256]{2,1,0:T(4,128)S(1)} %get-tuple-element.7, pred[256,256]{0,1:T(8,128)(4,1)S(1)} %get-tuple-element.13), kind=kOutput, calls=%fused_computation.14 | convolution fusion | flops 136314880 | bytes 3350528 | tf_op jit(solution)/shard_map/mjwh,hmn->mjwn/dot_general | solution.py:63
  70.9 0.9 %fusion.2 = (f32[2,4,256]{2,1,0:T(4,128)S(1)}, f32[2,4,256]{2,1,0:T(4,128)S(1)}) fusion(f32[2,256,256,4]{2,1,3,0:T(8,128)S(1)} %get-tuple-element.18, f32[2,4,256]{2,1,0:T(4,128)S(1)} %get-tuple-element.8, pred[256,256]{0,1:T(8,128)(4,1)S(1)} %get-tuple-element.14, f32[2,4,256]{2,1,0:T(4,128)S(1)} %get-tuple-element.7, ...), kind=kLoop, calls=%fused_computation.8 | loop fusion | flops 4190208 | bytes 4358144 | tf_op jit(solution)/shard_map/reduce_sum | solution.py:61
  72.1 1.4 %fusion.11 = f32[256,2,4,128]{3,0,2,1:T(8,128)S(1)} fusion(bf16[256,2,128,1]{0,2,3,1:T(8,128)(2,1)S(1)} %bitcast.133, f32[2,4,256,256]{2,3,1,0:T(8,128)S(1)} %get-tuple-element.20, f32[2,4,256]{2,1,0:T(4,128)S(1)} %get-tuple-element.11, f32[256,2,4]{0,2,1:T(4,128)S(1)} %get-tuple-element.9, f32[256,2,4]{0,2,1:T(4,128)S(1)} %get-tuple-element.10), kind=kOutput, calls=%fused_computation.20 | convolution fusion | flops 135790592 | bytes 3301376 | tf_op jit(solution)/shard_map/mjwh,hmn->mjwn/dot_general | solution.py:63
  73.5 2.1 %fusion.14 = bf16[256,2,4,128]{3,0,2,1:T(8,128)(2,1)S(1)} fusion(f32[256,2,4,128]{3,0,2,1:T(8,128)S(1)} %convolution_bitcast_fusion, f32[256,2,4,128]{3,0,2,1:T(8,128)S(1)} %fusion.11, bf16[256,2,128,1]{0,2,3,1:T(8,128)(2,1)} %bitcast.35, f32[2,256,256,4]{2,1,3,0:T(8,128)S(1)} %get-tuple-element.18, f32[2,4,256]{2,1,0:T(4,128)S(1)} %get-tuple-element.8, ...), kind=kOutput, calls=%fused_computation.24 | convolution fusion | flops 137625600 | bytes 4939776 | tf_op jit(solution)/shard_map/mjwh,hmn->mjwn/dot_general | solution.py:63
  75.7 0.4 copy.58
  76.5 5.1 %all_to_all.16 = bf16[2,128,1024]{2,1,0:T(8,128)(2,1)S(1)} all-to-all(bf16[2,128,1024]{2,1,0:T(8,128)(2,1)S(1)} %convert_element_type.32), channel_id=1, replica_groups=mesh['srv'=384,'head'=2] {'head'}, dimensions={0} | all-to-all | bytes 1048576 | tf_op jit(solution)/shard_map/all_to_all | solution.py:89
  81.8 1.0 %copy.60 = bf16[128,2048]{1,0:T(8,128)(2,1)} copy(bf16[128,2048]{0,1:T(8,128)(2,1)S(1)} %bitcast.132) | data formatting | bytes 1048576 | tf_op jit(solution)/shard_map/all_to_all | solution.py:89
  (24 shorter events, 1.4 us)
Async XLA Ops:
  6.5 34.4 %copy-start = (bf16[4096,256]{1,0:T(8,128)(2,1)S(1)}, bf16[4096,256]{1,0:T(8,128)(2,1)}, u32[]{:S(2)}) copy-start(bf16[4096,256]{1,0:T(8,128)(2,1)} %param.8) | copy-start | bytes 6291460
  6.5 34.4 %all-gather.3.cloned.1.call-start = ((), (), s32[]{:S(2)}) async-start(), calls=%async_computation.1 | async-start | bytes 3145728 | tf_op jit(solution)/shard_map/all_gather | solution.py:20
  19.4 2.7 %collective-permute-start.3 = (s32[256]{0:T(256)S(1)}, s32[256]{0:T(256)S(1)}, u32[]{:S(2)}, u32[]{:S(2)}) collective-permute-start(s32[256]{0:T(256)S(1)} %bitcast.135), channel_id=1, source_target_pairs={{0,4},{2,6},{4,8},{6,10},{8,12},{10,14},{12,16},{14,18},{16,20},{1... | collective-permute-start | bytes 3080 | tf_op jit(solution)/shard_map/ppermute | solution.py:15
  20.7 2.0 %collective-permute-start = (s32[256]{0:T(256)S(1)}, s32[256]{0:T(256)S(1)}, u32[]{:S(2)}, u32[]{:S(2)}) collective-permute-start(s32[256]{0:T(256)S(1)} %bitcast.136), channel_id=1, source_target_pairs={{0,2},{2,4},{4,6},{6,8},{8,10},{10,12},{12,14},{14,16},{16,18},{18... | collective-permute-start | bytes 3080 | tf_op jit(solution)/shard_map/ppermute | solution.py:15
  41.0 9.1 %copy-start.1 = (bf16[256,4096]{1,0:T(8,128)(2,1)S(1)}, bf16[256,4096]{1,0:T(8,128)(2,1)}, u32[]{:S(2)}) copy-start(bf16[256,4096]{1,0:T(8,128)(2,1)} %all-gather.3.cloned.1.call-done) | copy-start | bytes 6291460
  41.0 9.1 %copy-start.2 = (bf16[4096,256]{1,0:T(8,128)(2,1)S(1)}, bf16[4096,256]{1,0:T(8,128)(2,1)}, u32[]{:S(2)}) copy-start(bf16[4096,256]{1,0:T(8,128)(2,1)} %param.9) | copy-start | bytes 6291460
  43.6 22.6 %collective-permute-start.4 = (bf16[256,256]{0,1:T(8,128)(2,1)S(1)}, bf16[256,256]{0,1:T(8,128)(2,1)}, u32[]{:S(2)}, u32[]{:S(2)}) collective-permute-start(bf16[256,256]{0,1:T(8,128)(2,1)S(1)} %convolution_convert_fusion.2), channel_id=1, source_target_pairs={{0,4},{2,6},{4,8},{6,10},{8,12},{10,14},{12,16},{14,18},{16,20},{1... | collective-permute-start | bytes 393224 | tf_op jit(solution)/shard_map/ppermute | solution.py:15
  47.2 20.5 %collective-permute-start.1 = (bf16[256,256]{0,1:T(8,128)(2,1)S(1)}, bf16[256,256]{0,1:T(8,128)(2,1)}, u32[]{:S(2)}, u32[]{:S(2)}) collective-permute-start(bf16[256,256]{0,1:T(8,128)(2,1)S(1)} %convolution_convert_fusion.2), channel_id=1, source_target_pairs={{0,2},{2,4},{4,6},{6,8},{8,10},{10,12},{12,14},{14,16},{16,18},{18... | collective-permute-start | bytes 393224 | tf_op jit(solution)/shard_map/ppermute | solution.py:15
  51.0 18.2 %collective-permute-start.5 = (bf16[256,256]{0,1:T(8,128)(2,1)S(1)}, bf16[256,256]{0,1:T(8,128)(2,1)}, u32[]{:S(2)}, u32[]{:S(2)}) collective-permute-start(bf16[256,256]{0,1:T(8,128)(2,1)S(1)} %convolution_convert_fusion.1), channel_id=1, source_target_pairs={{0,4},{2,6},{4,8},{6,10},{8,12},{10,14},{12,16},{14,18},{16,20},{1... | collective-permute-start | bytes 393224 | tf_op jit(solution)/shard_map/ppermute | solution.py:15
  55.0 18.5 %collective-permute-start.2 = (bf16[256,256]{0,1:T(8,128)(2,1)S(1)}, bf16[256,256]{0,1:T(8,128)(2,1)}, u32[]{:S(2)}, u32[]{:S(2)}) collective-permute-start(bf16[256,256]{0,1:T(8,128)(2,1)S(1)} %convolution_convert_fusion.1), channel_id=1, source_target_pairs={{0,2},{2,4},{4,6},{6,8},{8,10},{10,12},{12,14},{14,16},{16,18},{18... | collective-permute-start | bytes 393224 | tf_op jit(solution)/shard_map/ppermute | solution.py:15
Sparse Core Ops, SparseCore 0:
  9.7 31.1 all-gather.2
where the time goes:
time: 90.1 us; the launch traced here: 89.7 us
  matrix products  18.9 us (21%)
  waiting for transfers between devices  18.5 us (21%)
  blocking collectives  17.2 us (19%)
  starting transfers between devices  16.7 us (19%)
  between operations  13.6 us (15%)
  local copies, waits for them, and re-layouts  2.43 us (3%)
  other arithmetic  2.41 us (3%)
    all_gather x1, waiting for transfers between devices, on_device(): lax.all_gather(tokens, 'head', axis=0, tiled=True)  17.2 us
    ppermute x6, starting transfers between devices, from_behind(): return lax.ppermute(x, axis, pairs)  16.7 us
    all_gather x1, blocking collectives, on_device(): lax.all_gather(doc_ids, 'head', axis=0, tiled=True)  12.1 us
    dot_general x1, matrix products, on_device(): jnp.dot(gathered, w_query, preferred_element_type=jnp.float32)  5.77 us
    dot_general x3, matrix products, attend(): jnp.einsum('mjwh,hmn->mjwn', attention_weight, value_block.reshape(group_...  5.16 us
    all_to_all x1, blocking collectives, on_device(): lax.all_to_all(result, 'head', split_axis=0, concat_axis=1, tiled=True)  5.11 us
    dot_general x3, matrix products, attend(): jnp.einsum('hfwl,afl->fwha', query_matrix, key_block.reshape(group_token,...  4.31 us
    dot_general x1, matrix products, on_device(): jnp.dot(gathered, w_key, preferred_element_type=jnp.float32)  2.66 us
  transfers between devices with their start and end apart: 7, of which 2 were waited for; matrix products, arithmetic and copies ran while one was open for 19% of the time, Pallas kernels for 0%

commit v1 on v0

v1 whole, which is shorter than its diff:
```python
import math

import jax
import jax.numpy as jnp
from jax import lax
from jax.experimental import pallas as pl
from jax.experimental.pallas import tpu as pltpu
from jax.sharding import PartitionSpec as P

HEAD_SIZE = 128
ROWS = 128
GROUP = 256
WIDTH = 4096
HEADS = 8
KV_HEADS = 2
SHARE = 4
KV = KV_HEADS * HEAD_SIZE
DOC_ROWS = 16
PAY_ROWS = 2 * KV_HEADS * GROUP + DOC_ROWS
Q_ROWS = HEADS * ROWS
DIGIT = 16
NEG = -1e30
SCALE = math.log2(math.e) / math.sqrt(HEAD_SIZE)
F32 = jnp.float32
BF16 = jnp.bfloat16


def dot(a, b):
    return jnp.dot(a, b, preferred_element_type=F32)


def dot_t(a, b):
    return lax.dot_general(a, b, (((1,), (1,)), ((), ())), preferred_element_type=F32)


def own_kv_kernel(own, w_key, w_value, docs, pay, ks, vs, xs, ids, sem, xsem):
    parts = sem.shape[1]
    step = WIDTH // parts
    first = [
        pltpu.make_async_copy(own, xs, xsem.at[0]),
        pltpu.make_async_copy(docs, ids, xsem.at[1]),
    ]
    copies = []
    for i in range(parts):
        cut = pl.ds(i * step, step)
        copies.append(
            [
                pltpu.make_async_copy(w_key.at[cut, :], ks.at[cut, :], sem.at[0, i]),
                pltpu.make_async_copy(w_value.at[cut, :], vs.at[cut, :], sem.at[1, i]),
            ]
        )
    for c in first + sum(copies, []):
        c.start()
    key = jnp.zeros((ROWS, KV), F32)
    value = jnp.zeros((ROWS, KV), F32)
    for c in first:
        c.wait()
    for i in range(parts):
        cut = pl.ds(i * step, step)
        x = xs[:, cut]
        copies[i][0].wait()
        key += dot(x, ks[cut, :])
        copies[i][1].wait()
        value += dot(x, vs[cut, :])
    for j in range(KV_HEADS):
        cols = slice(j * HEAD_SIZE, (j + 1) * HEAD_SIZE)
        pay[j * ROWS : (j + 1) * ROWS, :] = key[:, cols].astype(BF16)
        pay[(KV_HEADS + j) * ROWS : (KV_HEADS + j + 1) * ROWS, :] = value[:, cols].astype(BF16)
    doc = ids[...] + 1
    row = lax.broadcasted_iota(jnp.int32, (DOC_ROWS, ROWS), 0)
    digits = jnp.where(row == 0, doc // DIGIT, jnp.where(row == 1, doc % DIGIT, 0))
    pay[2 * KV_HEADS * ROWS :, :] = digits.astype(F32).astype(BF16)


def other_kv_kernel(other, own_pay, ks, vs, pay):
    x = other[...]
    parts = (dot(x, ks[...]).astype(BF16), dot(x, vs[...]).astype(BF16))
    for j in range(2 * KV_HEADS):
        pay[j * GROUP : j * GROUP + ROWS, :] = own_pay[j * ROWS : (j + 1) * ROWS, :]
        at = (j % KV_HEADS) * HEAD_SIZE
        pay[j * GROUP + ROWS : (j + 1) * GROUP, :] = parts[j // KV_HEADS][:, at : at + HEAD_SIZE]
    pay[2 * KV_HEADS * GROUP :, :] = own_pay[2 * KV_HEADS * ROWS :, :]


def query_kernel(own, other, w_query, pay, q_out, send, xs, ws, acc, sem, xsem):
    parts = sem.shape[0]
    step = WIDTH // parts
    ahead = 2
    x_copies = [
        pltpu.make_async_copy(own, xs.at[pl.ds(0, ROWS), :], xsem.at[0]),
        pltpu.make_async_copy(other, xs.at[pl.ds(ROWS, ROWS), :], xsem.at[1]),
    ]
    copies = []
    for i in range(parts):
        cut = pl.ds(i * step, step)
        copies.append(pltpu.make_async_copy(w_query.at[cut, :], ws.at[cut, :], sem.at[i]))
    for c in x_copies + copies[:ahead]:
        c.start()
    send[Q_ROWS:, :] = pay[...]
    for c in x_copies:
        c.wait()
    for i in range(parts):
        copies[i].wait()
        if i + ahead < parts:
            copies[i + ahead].start()
        cut = pl.ds(i * step, step)
        part = dot(xs[:, cut], ws[cut, :])
        if i == 0:
            acc[...] = part
        elif i < parts - 1:
            acc[...] += part
        else:
            q = (acc[...] + part).astype(BF16)
    for h in range(HEADS):
        rows = slice(h * ROWS, (h + 1) * ROWS)
        q_out[rows, :] = q[:ROWS, rows]
        send[rows, :] = q[ROWS:, rows]


def attend_kernel(q_mine, q_sent, pay, near_mine, near_sent, far_mine, far_sent, out):
    half = lax.axis_index("head")
    base = 2 * KV_HEADS * GROUP

    def ids(ref, start):
        d = ref[start + base : start + base + DOC_ROWS, :].astype(F32)
        return d[0:1] * DIGIT + d[1:2]

    docs = ids(pay, 0)
    doc_q = jnp.transpose(jnp.broadcast_to(docs, (ROWS, ROWS)))
    r = lax.broadcasted_iota(jnp.int32, (ROWS, ROWS), 0)
    c = lax.broadcasted_iota(jnp.int32, (ROWS, ROWS), 1)

    def bias(k):
        return jnp.where(doc_q == k, 0.0, NEG)

    flex_ids = jnp.where(half == 0, ids(far_sent, 0), ids(q_sent, Q_ROWS))
    biases = jnp.concatenate(
        [
            jnp.where((doc_q == docs) & (c <= r), 0.0, NEG),
            bias(ids(near_mine, 0)),
            bias(ids(near_sent, 0)),
            bias(ids(far_mine, 0)),
            bias(flex_ids),
        ],
        axis=1,
    )
    biases = jnp.concatenate([biases] * SHARE, axis=0)
    for side in range(2):
        q_ref = (q_mine, q_sent)[side]
        here, start = ((pay, 0), (q_sent, Q_ROWS))[side]
        near = (near_mine, near_sent)[side]
        far = (far_mine, far_sent)[side]
        mine, other = (0, ROWS) if side == 0 else (ROWS, 0)

        def gather(j):
            at = j * GROUP
            far_other = far[at + other : at + other + ROWS, :]
            here_other = here[start + at + other : start + at + other + ROWS, :]
            return jnp.concatenate(
                [
                    here[start + at + mine : start + at + mine + ROWS, :],
                    near[at + mine : at + mine + ROWS, :],
                    near[at + other : at + other + ROWS, :],
                    far[at + mine : at + mine + ROWS, :],
                    jnp.where(half == 0, far_other, here_other),
                ],
                axis=0,
            )

        for j in range(KV_HEADS):
            k = gather(j)
            v = gather(KV_HEADS + j)
            rows = slice(j * SHARE * ROWS, (j + 1) * SHARE * ROWS)
            s = dot_t(q_ref[rows, :], k) * SCALE + biases
            top = jnp.max(s, axis=1, keepdims=True)
            p = jnp.exp2(s - top)
            total = jnp.sum(p, axis=1, keepdims=True)
            o = (dot(p.astype(BF16), v) / total).astype(BF16)
            for i in range(SHARE):
                place = jnp.where(half == side, 0, HEADS) + j * SHARE + i
                cols = pl.ds(pl.multiple_of(place * HEAD_SIZE, HEAD_SIZE), HEAD_SIZE)
                out[:, cols] = o[i * ROWS : (i + 1) * ROWS, :]


VMEM = pl.BlockSpec(memory_space=pltpu.VMEM)
ANY = pl.BlockSpec(memory_space=pl.ANY)
DMA = pltpu.SemaphoreType.DMA


def call(kernel, name, outs, ins, mib, flops, size, scratch=()):
    many = isinstance(outs, list)
    return pl.pallas_call(
        kernel,
        out_shape=outs,
        in_specs=ins,
        out_specs=[VMEM] * len(outs) if many else VMEM,
        scratch_shapes=list(scratch),
        compiler_params=pltpu.CompilerParams(vmem_limit_bytes=mib << 20),
        cost_estimate=pl.CostEstimate(flops=flops, bytes_accessed=size, transcendentals=0),
        name=name,
    )


def bf16(*shape):
    return pltpu.VMEM(shape, BF16)


def stay(x):
    return pltpu.with_memory_space_constraint(x, pltpu.HBM)


def on_device(tokens, doc_ids, w_query, w_key, value_weight):
    groups = lax.axis_size("srv")

    def swap(x):
        return lax.ppermute(x, "head", [(0, 1), (1, 0)])

    other = swap(tokens)
    parts = 4
    own_pay, ks, vs = call(
        own_kv_kernel,
        "own_kv",
        [bf16(2 * KV_HEADS * ROWS + DOC_ROWS, HEAD_SIZE), bf16(WIDTH, KV), bf16(WIDTH, KV)],
        [ANY] * 4,
        16,
        4 * ROWS * WIDTH * KV,
        5 << 20,
        [
            pltpu.VMEM((ROWS, WIDTH), BF16),
            pltpu.VMEM((1, ROWS), jnp.int32),
            DMA((2, parts)),
            DMA((2,)),
        ],
    )(*map(stay, (tokens, w_key, value_weight, doc_ids.reshape(1, ROWS))))
    pay = call(
        other_kv_kernel,
        "other_kv",
        bf16(PAY_ROWS, HEAD_SIZE),
        [VMEM] * 4,
        16,
        4 * ROWS * WIDTH * KV,
        5 << 20,
    )(other, own_pay, ks, vs)
    near = lax.ppermute(pay, "srv", [(i, i + 1) for i in range(groups - 1)])
    far = lax.ppermute(pay, "srv", [(i, i + 2) for i in range(groups - 2)])
    q_mine, q_send = call(
        query_kernel,
        "query",
        [bf16(Q_ROWS, HEAD_SIZE), bf16(Q_ROWS + PAY_ROWS, HEAD_SIZE)],
        [ANY, ANY, ANY, VMEM],
        24,
        2 * GROUP * WIDTH * HEADS * HEAD_SIZE,
        11 << 20,
        [
            pltpu.VMEM((GROUP, WIDTH), BF16),
            pltpu.VMEM((WIDTH, HEADS * HEAD_SIZE), BF16),
            pltpu.VMEM((GROUP, HEADS * HEAD_SIZE), F32),
            DMA((parts,)),
            DMA((2,)),
        ],
    )(stay(tokens), other, stay(w_query), pay)
    q_sent = swap(q_send)
    near_sent = swap(near)
    far_sent = swap(far)
    return call(
        attend_kernel,
        "attend",
        jax.ShapeDtypeStruct((ROWS, 2 * HEADS * HEAD_SIZE), BF16),
        [VMEM] * 7,
        16,
        4 * ROWS * 5 * ROWS * 2 * HEADS * HEAD_SIZE,
        4 << 20,
    )(q_mine, q_sent, pay, near, near_sent, far, far_sent)


def solution(mesh):
    in_specs = (
        P(("srv", "head"), None),
        P(("srv", "head")),
        P(None, "head"),
        P(None, "head"),
        P(None, "head"),
    )
    out_specs = P(("srv", "head"), None)
    return jax.shard_map(
        on_device, mesh=mesh, in_specs=in_specs, out_specs=out_specs, check_vma=False
    )
```

time: 90.1 us -> 37.7 us (0.42)
  matrix products: 18.9 us -> 0 us
  blocking collectives: 17.2 us -> 0 us
  waiting for transfers between devices: 18.5 us -> 2.17 us
  between operations: 13.6 us -> 0.1 us
  Pallas kernels: 0 us -> 13.2 us
  starting transfers between devices: 16.7 us -> 21.8 us
  local copies, waits for them, and re-layouts: 2.43 us -> 0 us
  other arithmetic: 2.41 us -> 0 us
    dot_general x9 -> x0, matrix products: 18.9 us -> none  [the longest x1 5.77 us: on_device(): jnp.dot(gathered, w_query, preferred_element_type=jnp.float32)]
    all_gather x1 -> x0, waiting for transfers between devices: 17.2 us -> none  [on_device(): lax.all_gather(tokens, 'head', axis=0, tiled=True)]
    pallas_call x0 -> x4, Pallas kernels: none -> 13.2 us  [the longest x1 5.05 us: on_device(): call(query_kernel, 'query', [bf16(Q_ROWS, HEAD_SIZE), bf16(Q_ROWS + PAY_R...]
    all_gather x1 -> x0, blocking collectives: 12.1 us -> none  [on_device(): lax.all_gather(doc_ids, 'head', axis=0, tiled=True)]
    ppermute x6, starting transfers between devices: 16.7 us -> 21.8 us  [the longest x4 19.2 us: swap(): return lax.ppermute(x, 'head', [(0, 1), (1, 0)])]
    all_to_all x1 -> x0, blocking collectives: 5.11 us -> none  [on_device(): lax.all_to_all(result, 'head', split_axis=0, concat_axis=1, tiled=True)]
    ppermute x6, waiting for transfers between devices: 0.62 us -> 2.17 us  [the longest x4 1.13 us: swap(): return lax.ppermute(x, 'head', [(0, 1), (1, 0)])]
    all_to_all x2 -> x0, local copies, waits for them, and re-layouts: 1.28 us -> none  [on_device(): lax.all_to_all(result, 'head', split_axis=0, concat_axis=1, tiled=True)]
  transfers between devices with their start and end apart: 7 -> 6, of which waited for: 2 -> 2; matrix products, arithmetic and copies ran while one was open for 19% -> 0% of each run, Pallas kernels for 0% -> 24%
where the time goes in v1:
time: 37.7 us; the launch traced here: 37.3 us
  starting transfers between devices  21.8 us (58%)
  Pallas kernels  13.2 us (35%)
  waiting for transfers between devices  2.17 us (6%)
    ppermute x4, starting transfers between devices, swap(): return lax.ppermute(x, 'head', [(0, 1), (1, 0)])  19.2 us
    pallas_call x1, Pallas kernels, on_device(): call(query_kernel, 'query', [bf16(Q_ROWS, HEAD_SIZE), bf16(Q_ROWS + PAY_R...  5.05 us
    pallas_call x1, Pallas kernels, on_device(): call(own_kv_kernel, 'own_kv', [bf16(2 * KV_HEADS * ROWS + DOC_ROWS, HEAD_...  3.93 us
    pallas_call x1, Pallas kernels, on_device(): call(attend_kernel, 'attend', jax.ShapeDtypeStruct((ROWS, 2 * HEADS * HEA...  3.47 us
    ppermute x1, starting transfers between devices, on_device(): near = lax.ppermute(pay, 'srv', [(i, i + 1) for i in range(groups - 1)])  1.31 us
    ppermute x1, starting transfers between devices, on_device(): far = lax.ppermute(pay, 'srv', [(i, i + 2) for i in range(groups - 2)])  1.31 us
    ppermute x4, waiting for transfers between devices, swap(): return lax.ppermute(x, 'head', [(0, 1), (1, 0)])  1.13 us
    ppermute x1, waiting for transfers between devices, on_device(): near = lax.ppermute(pay, 'srv', [(i, i + 1) for i in range(groups - 1)])  1.03 us
  transfers between devices with their start and end apart: 6, of which 2 were waited for; matrix products, arithmetic and copies ran while one was open for 0% of the time, Pallas kernels for 24%

profile of v1, /device:TPU:1, one launch (start us, length us, event | category | flops | bytes accessed | tf_op | source)
XLA Modules:
  0.0 37.3 jit_solution(2726997369551832463)
XLA Ops:
  0.0 12.4 %collective-permute-start = (bf16[128,4096]{1,0:T(8,128)(2,1)}, bf16[128,4096]{1,0:T(8,128)(2,1)S(1)}, u32[]{:S(2)}, u32[]{:S(2)}) collective-permute-start(bf16[128,4096]{1,0:T(8,128)(2,1)} %own.3), channel_id=1, source_target_pairs={{0,1},{1,0},{2,3},{3,2},{4,5},{5,4},{6,7},{7,6},{8,9},{9,8},{10,11... | collective-permute-start | bytes 3145736 | tf_op jit(solution)/shard_map/ppermute | solution.py:216
  12.4 3.9 %own_kv.1 = (bf16[528,128]{1,0:T(8,128)(2,1)S(1)}, bf16[4096,256]{1,0:T(8,128)(2,1)S(1)}, bf16[4096,256]{1,0:T(8,128)(2,1)S(1)}) custom-call(bf16[128,4096]{1,0:T(8,128)(2,1)} %own.3, bf16[4096,256]{1,0:T(8,128)(2,1)} %w_key.1, bf16[4096,256]{1,0:T(8,128)(2,1)} %w_value.1, s32[1,128]{1,0:T(1,128)} %bitcast.1), custom_call_target="tpu_custom_call" | custom-call | flops 536870912 | bytes 5242880 | tf_op jit(solution)/shard_map/own_kv/pallas_call | solution.py:220
  16.4 0.0 collective-permute-done.other
  16.4 0.8 %other_kv.1.pay = bf16[1040,128]{1,0:T(8,128)(2,1)S(1)} custom-call(bf16[128,4096]{1,0:T(8,128)(2,1)S(1)} %collective-permute-done.other, bf16[528,128]{1,0:T(8,128)(2,1)S(1)} %get-tuple-element.10.own_pay, bf16[4096,256]{1,0:T(8,128)(2,1)S(1)} %get-tuple-element.11.ks, bf16[4096,256]{1,0:T(8,128)(2,1)S(1)} %get-tuple-element.12.vs), custom_call_target="tpu_custom_call" | custom-call | flops 536870912 | bytes 5242880 | tf_op jit(solution)/shard_map/other_kv/pallas_call | solution.py:235
  17.1 1.3 %collective-permute-start.4 = (bf16[1040,128]{1,0:T(8,128)(2,1)S(1)}, bf16[1040,128]{1,0:T(8,128)(2,1)S(1)}, u32[]{:S(2)}, u32[]{:S(2)}) collective-permute-start(bf16[1040,128]{1,0:T(8,128)(2,1)S(1)} %other_kv.1.pay), channel_id=1, source_target_pairs={{0,4},{2,6},{4,8},{6,10},{8,12},{10,14},{12,16},{14,18},{16,20},{1... | collective-permute-start | bytes 798728 | tf_op jit(solution)/shard_map/ppermute | solution.py:245
  18.4 1.3 %collective-permute-start.2 = (bf16[1040,128]{1,0:T(8,128)(2,1)S(1)}, bf16[1040,128]{1,0:T(8,128)(2,1)S(1)}, u32[]{:S(2)}, u32[]{:S(2)}) collective-permute-start(bf16[1040,128]{1,0:T(8,128)(2,1)S(1)} %other_kv.1.pay), channel_id=1, source_target_pairs={{0,2},{2,4},{4,6},{6,8},{8,10},{10,12},{12,14},{14,16},{16,18},{18... | collective-permute-start | bytes 798728 | tf_op jit(solution)/shard_map/ppermute | solution.py:244
  19.8 5.0 %query.1 = (bf16[1024,128]{1,0:T(8,128)(2,1)S(1)}, bf16[2064,128]{1,0:T(8,128)(2,1)S(1)}) custom-call(bf16[128,4096]{1,0:T(8,128)(2,1)} %own.3, bf16[128,4096]{1,0:T(8,128)(2,1)S(1)} %collective-permute-done.other, bf16[4096,1024]{1,0:T(8,128)(2,1)} %w_query.1, bf16[1040,128]{1,0:T(8,128)(2,1)S(1)} %other_kv.1.pay), custom_call_target="tpu_custom_call" | custom-call | flops 2147483648 | bytes 11534336 | tf_op jit(solution)/shard_map/query/pallas_call | solution.py:246
  24.8 1.9 %collective-permute-start.1 = (bf16[2064,128]{1,0:T(8,128)(2,1)S(1)}, bf16[2064,128]{1,0:T(8,128)(2,1)S(1)}, u32[]{:S(2)}, u32[]{:S(2)}) collective-permute-start(bf16[2064,128]{1,0:T(8,128)(2,1)S(1)} %get-tuple-element.14), channel_id=1, source_target_pairs={{0,1},{1,0},{2,3},{3,2},{4,5},{5,4},{6,7},{7,6},{8,9},{9,8},{10,11... | collective-permute-start | bytes 1585160 | tf_op jit(solution)/shard_map/ppermute | solution.py:216
  26.7 0.0 collective-permute-done.4.far_mine
  26.8 2.4 %collective-permute-start.5 = (bf16[1040,128]{1,0:T(8,128)(2,1)S(1)}, bf16[1040,128]{1,0:T(8,128)(2,1)S(1)}, u32[]{:S(2)}, u32[]{:S(2)}) collective-permute-start(bf16[1040,128]{1,0:T(8,128)(2,1)S(1)} %collective-permute-done.4.far_mine), channel_id=1, source_target_pairs={{0,1},{1,0},{2,3},{3,2},{4,5},{5,4},{6,7},{7,6},{8,9},{9,8},{10,11... | collective-permute-start | bytes 798728 | tf_op jit(solution)/shard_map/ppermute | solution.py:216
  29.2 1.0 %collective-permute-done.2.near_mine = bf16[1040,128]{1,0:T(8,128)(2,1)S(1)} collective-permute-done((bf16[1040,128]{1,0:T(8,128)(2,1)S(1)}, bf16[1040,128]{1,0:T(8,128)(2,1)S(1)}, u32[]{:S(2)}, u32[]{:S(2)}) %collective-permute-start.2) | collective-permute-done | bytes 266272 | tf_op jit(solution)/shard_map/ppermute | solution.py:244
  30.2 2.5 %collective-permute-start.3 = (bf16[1040,128]{1,0:T(8,128)(2,1)S(1)}, bf16[1040,128]{1,0:T(8,128)(2,1)S(1)}, u32[]{:S(2)}, u32[]{:S(2)}) collective-permute-start(bf16[1040,128]{1,0:T(8,128)(2,1)S(1)} %collective-permute-done.2.near_mine), channel_id=1, source_target_pairs={{0,1},{1,0},{2,3},{3,2},{4,5},{5,4},{6,7},{7,6},{8,9},{9,8},{10,11... | collective-permute-start | bytes 798728 | tf_op jit(solution)/shard_map/ppermute | solution.py:216
  32.7 0.0 collective-permute-done.1.q_sent
  32.7 0.0 collective-permute-done.5.far_sent
  32.7 1.1 %collective-permute-done.3.near_sent = bf16[1040,128]{1,0:T(8,128)(2,1)S(1)} collective-permute-done((bf16[1040,128]{1,0:T(8,128)(2,1)S(1)}, bf16[1040,128]{1,0:T(8,128)(2,1)S(1)}, u32[]{:S(2)}, u32[]{:S(2)}) %collective-permute-start.3) | collective-permute-done | bytes 266272 | tf_op jit(solution)/shard_map/ppermute | solution.py:216
  33.8 3.5 %attend.1 = bf16[128,2048]{1,0:T(8,128)(2,1)} custom-call(bf16[1024,128]{1,0:T(8,128)(2,1)S(1)} %get-tuple-element.13.q_mine, bf16[2064,128]{1,0:T(8,128)(2,1)S(1)} %collective-permute-done.1.q_sent, bf16[1040,128]{1,0:T(8,128)(2,1)S(1)} %other_kv.1.pay, bf16[1040,128]{1,0:T(8,128)(2,1)S(1)} %collective-permute-done.2.near_mine, ...), custom_call_target="tpu_custom_call" | custom-call | flops 671088640 | bytes 4194304 | tf_op jit(solution)/shard_map/attend/pallas_call | solution.py:265
Async XLA Ops:
  0.0 16.4 %collective-permute-start = (bf16[128,4096]{1,0:T(8,128)(2,1)}, bf16[128,4096]{1,0:T(8,128)(2,1)S(1)}, u32[]{:S(2)}, u32[]{:S(2)}) collective-permute-start(bf16[128,4096]{1,0:T(8,128)(2,1)} %own.3), channel_id=1, source_target_pairs={{0,1},{1,0},{2,3},{3,2},{4,5},{5,4},{6,7},{7,6},{8,9},{9,8},{10,11... | collective-permute-start | bytes 3145736 | tf_op jit(solution)/shard_map/ppermute | solution.py:216
  17.1 9.6 %collective-permute-start.4 = (bf16[1040,128]{1,0:T(8,128)(2,1)S(1)}, bf16[1040,128]{1,0:T(8,128)(2,1)S(1)}, u32[]{:S(2)}, u32[]{:S(2)}) collective-permute-start(bf16[1040,128]{1,0:T(8,128)(2,1)S(1)} %other_kv.1.pay), channel_id=1, source_target_pairs={{0,4},{2,6},{4,8},{6,10},{8,12},{10,14},{12,16},{14,18},{16,20},{1... | collective-permute-start | bytes 798728 | tf_op jit(solution)/shard_map/ppermute | solution.py:245
  18.4 11.8 %collective-permute-start.2 = (bf16[1040,128]{1,0:T(8,128)(2,1)S(1)}, bf16[1040,128]{1,0:T(8,128)(2,1)S(1)}, u32[]{:S(2)}, u32[]{:S(2)}) collective-permute-start(bf16[1040,128]{1,0:T(8,128)(2,1)S(1)} %other_kv.1.pay), channel_id=1, source_target_pairs={{0,2},{2,4},{4,6},{6,8},{8,10},{10,12},{12,14},{14,16},{16,18},{18... | collective-permute-start | bytes 798728 | tf_op jit(solution)/shard_map/ppermute | solution.py:244
  24.8 7.9 %collective-permute-start.1 = (bf16[2064,128]{1,0:T(8,128)(2,1)S(1)}, bf16[2064,128]{1,0:T(8,128)(2,1)S(1)}, u32[]{:S(2)}, u32[]{:S(2)}) collective-permute-start(bf16[2064,128]{1,0:T(8,128)(2,1)S(1)} %get-tuple-element.14), channel_id=1, source_target_pairs={{0,1},{1,0},{2,3},{3,2},{4,5},{5,4},{6,7},{7,6},{8,9},{9,8},{10,11... | collective-permute-start | bytes 1585160 | tf_op jit(solution)/shard_map/ppermute | solution.py:216
  26.8 5.9 %collective-permute-start.5 = (bf16[1040,128]{1,0:T(8,128)(2,1)S(1)}, bf16[1040,128]{1,0:T(8,128)(2,1)S(1)}, u32[]{:S(2)}, u32[]{:S(2)}) collective-permute-start(bf16[1040,128]{1,0:T(8,128)(2,1)S(1)} %collective-permute-done.4.far_mine), channel_id=1, source_target_pairs={{0,1},{1,0},{2,3},{3,2},{4,5},{5,4},{6,7},{7,6},{8,9},{9,8},{10,11... | collective-permute-start | bytes 798728 | tf_op jit(solution)/shard_map/ppermute | solution.py:216
  30.2 3.6 %collective-permute-start.3 = (bf16[1040,128]{1,0:T(8,128)(2,1)S(1)}, bf16[1040,128]{1,0:T(8,128)(2,1)S(1)}, u32[]{:S(2)}, u32[]{:S(2)}) collective-permute-start(bf16[1040,128]{1,0:T(8,128)(2,1)S(1)} %collective-permute-done.2.near_mine), channel_id=1, source_target_pairs={{0,1},{1,0},{2,3},{3,2},{4,5},{5,4},{6,7},{7,6},{8,9},{9,8},{10,11... | collective-permute-start | bytes 798728 | tf_op jit(solution)/shard_map/ppermute | solution.py:216

commit v2 on v1

v2 whole, which is shorter than its diff:
```python
import math

import jax
import jax.numpy as jnp
from jax import lax
from jax.experimental import pallas as pl
from jax.experimental.pallas import tpu as pltpu
from jax.sharding import PartitionSpec as P

HEAD_SIZE = 128
ROWS = 128
GROUP = 256
WIDTH = 4096
HEADS = 8
KV_HEADS = 2
SHARE = 4
KV = KV_HEADS * HEAD_SIZE
DOC_ROWS = 16
PAY_ROWS = 2 * KV_HEADS * GROUP + DOC_ROWS
Q_ROWS = HEADS * ROWS
DIGIT = 16
NEG = -1e30
SCALE = math.log2(math.e) / math.sqrt(HEAD_SIZE)
F32 = jnp.float32
BF16 = jnp.bfloat16


def dot(a, b):
    return jnp.dot(a, b, preferred_element_type=F32)


def dot_t(a, b):
    return lax.dot_general(a, b, (((1,), (1,)), ((), ())), preferred_element_type=F32)


def first_kernel(out):
    out[...] = jnp.zeros_like(out)


def own_kv_kernel(first, own, w_key, w_value, docs, pay):
    x = own[...]
    key = dot(x, w_key[...])
    value = dot(x, w_value[...])
    for j in range(KV_HEADS):
        cols = slice(j * HEAD_SIZE, (j + 1) * HEAD_SIZE)
        pay[j * ROWS : (j + 1) * ROWS, :] = key[:, cols].astype(BF16)
        pay[(KV_HEADS + j) * ROWS : (KV_HEADS + j + 1) * ROWS, :] = value[:, cols].astype(BF16)
    doc = docs[...] + 1
    row = lax.broadcasted_iota(jnp.int32, (DOC_ROWS, ROWS), 0)
    digits = jnp.where(row == 0, doc // DIGIT, jnp.where(row == 1, doc % DIGIT, 0))
    pay[2 * KV_HEADS * ROWS :, :] = digits.astype(F32).astype(BF16)


def other_kv_kernel(other, own_pay, ks, vs, pay):
    x = other[...]
    parts = (dot(x, ks[...]).astype(BF16), dot(x, vs[...]).astype(BF16))
    for j in range(2 * KV_HEADS):
        pay[j * GROUP : j * GROUP + ROWS, :] = own_pay[j * ROWS : (j + 1) * ROWS, :]
        at = (j % KV_HEADS) * HEAD_SIZE
        pay[j * GROUP + ROWS : (j + 1) * GROUP, :] = parts[j // KV_HEADS][:, at : at + HEAD_SIZE]
    pay[2 * KV_HEADS * GROUP :, :] = own_pay[2 * KV_HEADS * ROWS :, :]


def query_kernel(own, other, w_query, pay, q_out, send):
    step = 2 * HEAD_SIZE
    send[Q_ROWS:, :] = pay[...]
    for i in range(HEADS // 2):
        w = w_query[:, i * step : (i + 1) * step]
        mine = dot(own[...], w).astype(BF16)
        theirs = dot(other[...], w).astype(BF16)
        for j in range(2):
            rows = pl.ds((2 * i + j) * ROWS, ROWS)
            cols = slice(j * HEAD_SIZE, (j + 1) * HEAD_SIZE)
            q_out[rows, :] = mine[:, cols]
            send[rows, :] = theirs[:, cols]


BASE = 2 * KV_HEADS * GROUP


def ids_of(ref, start=0):
    d = ref[start + BASE : start + BASE + DOC_ROWS, :].astype(F32)
    return d[0:1] * DIGIT + d[1:2]


def down(ids):
    return jnp.transpose(jnp.broadcast_to(ids, (ROWS, ROWS)))


def tall(*blocks):
    return jnp.concatenate([jnp.concatenate(blocks, axis=1)] * SHARE, axis=0)


def wide(x):
    return jnp.broadcast_to(x, (SHARE * ROWS, HEAD_SIZE))


def near_kernel(q_mine, q_sent, pay, near_mine, near_sent, acc_out, m_out, l_out):
    half = lax.axis_index("head")
    docs = ids_of(pay)
    doc_q = down(docs)
    r = lax.broadcasted_iota(jnp.int32, (ROWS, ROWS), 0)
    c = lax.broadcasted_iota(jnp.int32, (ROWS, ROWS), 1)
    here_mine = jnp.where((doc_q == docs) & (c <= r), 0.0, NEG)
    here_other = jnp.where((doc_q == ids_of(q_sent, Q_ROWS)) & (c < half * ROWS), 0.0, NEG)
    near_a = jnp.where(doc_q == ids_of(near_mine), 0.0, NEG)
    near_b = jnp.where(doc_q == ids_of(near_sent), 0.0, NEG)
    for side in range(2):
        if side == 0:
            q_ref, here, start, near = q_mine, pay, 0, near_mine
            bias = tall(here_mine, here_other, near_a, near_b)
        else:
            q_ref, here, start, near = q_sent, q_sent, Q_ROWS, near_sent
            bias = tall(here_other, here_mine, near_b, near_a)
        for j in range(KV_HEADS):
            rows = pl.ds(j * SHARE * ROWS, SHARE * ROWS)
            k_at = j * GROUP
            v_at = (KV_HEADS + j) * GROUP
            k = jnp.concatenate([here[pl.ds(start + k_at, GROUP), :], near[pl.ds(k_at, GROUP), :]], axis=0)
            v = jnp.concatenate([here[pl.ds(start + v_at, GROUP), :], near[pl.ds(v_at, GROUP), :]], axis=0)
            s = dot_t(q_ref[rows, :], k) * SCALE + bias
            top = jnp.max(s, axis=1, keepdims=True)
            p = jnp.exp2(s - top)
            to = pl.ds((side * HEADS + j * SHARE) * ROWS, SHARE * ROWS)
            m_out[to, :] = wide(top)
            l_out[to, :] = wide(jnp.sum(p, axis=1, keepdims=True))
            acc_out[to, :] = dot(p.astype(BF16), v)


def far_kernel(q_mine, q_sent, pay, far_mine, far_sent, acc_in, m_in, l_in, out, buf, sem):
    half = lax.axis_index("head")
    doc_q = down(ids_of(pay))
    far_a = jnp.where(doc_q == ids_of(far_mine), 0.0, NEG)
    far_b = jnp.where(doc_q == ids_of(far_sent), 0.0, NEG)
    copies = []
    for side in range(2):
        q_ref = (q_mine, q_sent)[side]
        far = (far_mine, far_sent)[side]
        bias = tall(far_a, far_b) if side == 0 else tall(far_b, far_a)
        for j in range(KV_HEADS):
            rows = pl.ds(j * SHARE * ROWS, SHARE * ROWS)
            at = pl.ds((side * HEADS + j * SHARE) * ROWS, SHARE * ROWS)
            s = dot_t(q_ref[rows, :], far[pl.ds(j * GROUP, GROUP), :]) * SCALE + bias
            old = m_in[at, :]
            top = jnp.maximum(old, wide(jnp.max(s, axis=1, keepdims=True)))
            factor = jnp.exp2(old - top)
            p = jnp.exp2(s - jnp.concatenate([top, top], axis=1))
            total = l_in[at, :] * factor + wide(jnp.sum(p, axis=1, keepdims=True))
            acc = acc_in[at, :] * factor
            acc += dot(p.astype(BF16), far[pl.ds((KV_HEADS + j) * GROUP, GROUP), :])
            o = (acc / total).astype(BF16)
            for i in range(SHARE):
                col = (j * SHARE + i) * HEAD_SIZE
                buf[side, :, col : col + HEAD_SIZE] = o[i * ROWS : (i + 1) * ROWS, :]
        width = HEADS * HEAD_SIZE
        start = pl.multiple_of(jnp.where(half == side, 0, width), width)
        copy = pltpu.make_async_copy(buf.at[side], out.at[:, pl.ds(start, width)], sem.at[side])
        copy.start()
        copies.append(copy)
    for copy in copies:
        copy.wait()


VMEM = pl.BlockSpec(memory_space=pltpu.VMEM)
ANY = pl.BlockSpec(memory_space=pl.ANY)
DMA = pltpu.SemaphoreType.DMA


def call(kernel, name, outs, ins, mib, flops, size, scratch=(), to=None):
    many = isinstance(outs, list)
    return pl.pallas_call(
        kernel,
        out_shape=outs,
        in_specs=ins,
        out_specs=[VMEM] * len(outs) if many else to or VMEM,
        scratch_shapes=list(scratch),
        compiler_params=pltpu.CompilerParams(vmem_limit_bytes=mib << 20),
        cost_estimate=pl.CostEstimate(flops=flops, bytes_accessed=size, transcendentals=0),
        name=name,
    )


def bf16(*shape):
    return pltpu.VMEM(shape, BF16)


def fast(x):
    return pltpu.with_memory_space_constraint(x, pltpu.VMEM)


def on_device(tokens, doc_ids, w_query, w_key, value_weight):
    groups = lax.axis_size("srv")

    def swap(x):
        return lax.ppermute(x, "head", [(0, 1), (1, 0)])

    first = call(first_kernel, "first", bf16(DOC_ROWS, HEAD_SIZE), [], 1, 10**11, 10**11)()
    own, w_query, w_key, w_value = map(fast, (tokens, w_query, w_key, value_weight))
    other = swap(tokens)
    flops = 4 * ROWS * WIDTH * KV
    own_pay = call(
        own_kv_kernel,
        "own_kv",
        bf16(2 * KV_HEADS * ROWS + DOC_ROWS, HEAD_SIZE),
        [ANY] + [VMEM] * 4,
        16,
        flops,
        5 << 20,
    )(first, own, w_key, w_value, doc_ids.reshape(1, ROWS))
    pay = call(
        other_kv_kernel, "other_kv", bf16(PAY_ROWS, HEAD_SIZE), [VMEM] * 4, 16, flops, 5 << 20
    )(other, own_pay, w_key, w_value)
    near = lax.ppermute(pay, "srv", [(i, i + 1) for i in range(groups - 1)])
    far = lax.ppermute(pay, "srv", [(i, i + 2) for i in range(groups - 2)])
    q_mine, q_send = call(
        query_kernel,
        "query",
        [bf16(Q_ROWS, HEAD_SIZE), bf16(Q_ROWS + PAY_ROWS, HEAD_SIZE)],
        [VMEM] * 4,
        24,
        2 * GROUP * WIDTH * HEADS * HEAD_SIZE,
        11 << 20,
    )(own, other, w_query, pay)
    q_sent = swap(q_send)
    near_sent = swap(near)
    far_sent = swap(far)
    pairs = ROWS * GROUP * 2 * HEADS * HEAD_SIZE
    acc, m, l = call(
        near_kernel,
        "attend_near",
        [pltpu.VMEM((2 * Q_ROWS, n), F32) for n in [HEAD_SIZE] * 3],
        [VMEM] * 5,
        16,
        1,
        1,
    )(q_mine, q_sent, pay, near, near_sent)
    return call(
        far_kernel,
        "attend_far",
        jax.ShapeDtypeStruct((ROWS, 2 * HEADS * HEAD_SIZE), BF16),
        [VMEM] * 8,
        16,
        4 * pairs,
        4 << 20,
        [pltpu.VMEM((2, ROWS, HEADS * HEAD_SIZE), BF16), DMA((2,))],
        ANY,
    )(q_mine, q_sent, pay, far, far_sent, acc, m, l)


def solution(mesh):
    in_specs = (
        P(("srv", "head"), None),
        P(("srv", "head")),
        P(None, "head"),
        P(None, "head"),
        P(None, "head"),
    )
    out_specs = P(("srv", "head"), None)
    return jax.shard_map(
        on_device, mesh=mesh, in_specs=in_specs, out_specs=out_specs, check_vma=False
    )
```

time: 37.7 us -> 35.4 us (0.939)
  Pallas kernels: 13.2 us -> 7.39 us
  waiting for transfers between devices: 2.17 us -> 4.1 us
  starting transfers between devices: 21.8 us -> 23.2 us
    pallas_call x2 -> x4, Pallas kernels: 7.41 us -> 4.23 us  [the longest x1 1.82 us: on_device(): call(far_kernel, 'attend_far', jax.ShapeDtypeStruct((ROWS, 2 * HEADS * HE...]
    pallas_call x1, Pallas kernels: 5.05 us -> 2.43 us  [on_device(): call(query_kernel, 'query', [bf16(Q_ROWS, HEAD_SIZE), bf16(Q_ROWS + PAY_R...]
    ppermute x1, waiting for transfers between devices: 0.01 us -> 2.42 us  [on_device(): far = lax.ppermute(pay, 'srv', [(i, i + 2) for i in range(groups - 2)])]
    ppermute x4, starting transfers between devices: 19.2 us -> 20.6 us  [swap(): return lax.ppermute(x, 'head', [(0, 1), (1, 0)])]
    ppermute x1, waiting for transfers between devices: 1.03 us -> 0.01 us  [on_device(): near = lax.ppermute(pay, 'srv', [(i, i + 1) for i in range(groups - 1)])]
    ppermute x4, waiting for transfers between devices: 1.13 us -> 1.67 us  [swap(): return lax.ppermute(x, 'head', [(0, 1), (1, 0)])]
  transfers between devices with their start and end apart: 6 -> 6, of which waited for: 2 -> 2; matrix products, arithmetic and copies ran while one was open for 0% -> 0% of each run, Pallas kernels for 24% -> 14%
where the time goes in v2:
time: 35.4 us; the launch traced here: 34.9 us
  starting transfers between devices  23.2 us (66%)
  Pallas kernels  7.39 us (21%)
  waiting for transfers between devices  4.1 us (12%)
    ppermute x4, starting transfers between devices, swap(): return lax.ppermute(x, 'head', [(0, 1), (1, 0)])  20.6 us
    pallas_call x1, Pallas kernels, on_device(): call(query_kernel, 'query', [bf16(Q_ROWS, HEAD_SIZE), bf16(Q_ROWS + PAY_R...  2.43 us
    ppermute x1, waiting for transfers between devices, on_device(): far = lax.ppermute(pay, 'srv', [(i, i + 2) for i in range(groups - 2)])  2.42 us
    pallas_call x1, Pallas kernels, on_device(): call(far_kernel, 'attend_far', jax.ShapeDtypeStruct((ROWS, 2 * HEADS * HE...  1.82 us
    ppermute x4, waiting for transfers between devices, swap(): return lax.ppermute(x, 'head', [(0, 1), (1, 0)])  1.67 us
    pallas_call x1, Pallas kernels, on_device(): call(near_kernel, 'attend_near', [pltpu.VMEM((2 * Q_ROWS, n), F32) for n...  1.65 us
    ppermute x1, starting transfers between devices, on_device(): far = lax.ppermute(pay, 'srv', [(i, i + 2) for i in range(groups - 2)])  1.31 us
    ppermute x1, starting transfers between devices, on_device(): near = lax.ppermute(pay, 'srv', [(i, i + 1) for i in range(groups - 1)])  1.31 us
  transfers between devices with their start and end apart: 6, of which 2 were waited for; matrix products, arithmetic and copies ran while one was open for 0% of the time, Pallas kernels for 14%

profile of v2, /device:TPU:1, one launch (start us, length us, event | category | flops | bytes accessed | tf_op | source)
XLA Modules:
  0.0 34.9 jit_solution(11367778835365244031)
XLA Ops:
  0.0 0.0 copy-start.2
  0.0 12.7 %collective-permute-start = (bf16[128,4096]{1,0:T(8,128)(2,1)}, bf16[128,4096]{1,0:T(8,128)(2,1)S(1)}, u32[]{:S(2)}, u32[]{:S(2)}) collective-permute-start(bf16[128,4096]{1,0:T(8,128)(2,1)} %own.3), channel_id=1, source_target_pairs={{0,1},{1,0},{2,3},{3,2},{4,5},{5,4},{6,7},{7,6},{8,9},{9,8},{10,11... | collective-permute-start | bytes 3145736 | tf_op jit(solution)/shard_map/ppermute | solution.py:195
  12.7 0.0 copy-done.3
  12.7 0.0 copy-done.4
  12.7 0.0 copy-done.1
  12.7 0.0 copy-done.2
  12.7 0.0 copy-start
  12.8 0.7 %own_kv.1.own_pay = bf16[528,128]{1,0:T(8,128)(2,1)S(1)} custom-call(bf16[16,128]{1,0:T(8,128)(2,1)S(1)} %first.1, bf16[128,4096]{1,0:T(8,128)(2,1)S(1)} %copy-done.3, bf16[4096,256]{1,0:T(8,128)(2,1)S(1)} %copy-done.1, bf16[4096,256]{1,0:T(8,128)(2,1)S(1)} %copy-done.2, s32[1,128]{1,0:T(1,128)S(1)} %bitcast.1), custom_call_target="tpu_custom_call" | custom-call | flops 536870912 | bytes 5242880 | tf_op jit(solution)/shard_map/own_kv/pallas_call | solution.py:201
  13.5 1.7 %collective-permute-done.other = bf16[128,4096]{1,0:T(8,128)(2,1)S(1)} collective-permute-done((bf16[128,4096]{1,0:T(8,128)(2,1)}, bf16[128,4096]{1,0:T(8,128)(2,1)S(1)}, u32[]{:S(2)}, u32[]{:S(2)}) %collective-permute-start) | collective-permute-done | bytes 1048608 | tf_op jit(solution)/shard_map/ppermute | solution.py:195
  15.2 0.7 %other_kv.1.pay = bf16[1040,128]{1,0:T(8,128)(2,1)S(1)} custom-call(bf16[128,4096]{1,0:T(8,128)(2,1)S(1)} %collective-permute-done.other, bf16[528,128]{1,0:T(8,128)(2,1)S(1)} %own_kv.1.own_pay, bf16[4096,256]{1,0:T(8,128)(2,1)S(1)} %copy-done.1, bf16[4096,256]{1,0:T(8,128)(2,1)S(1)} %copy-done.2), custom_call_target="tpu_custom_call" | custom-call | flops 536870912 | bytes 5242880 | tf_op jit(solution)/shard_map/other_kv/pallas_call | solution.py:210
  15.9 1.3 %collective-permute-start.4 = (bf16[1040,128]{1,0:T(8,128)(2,1)S(1)}, bf16[1040,128]{1,0:T(8,128)(2,1)S(1)}, u32[]{:S(2)}, u32[]{:S(2)}) collective-permute-start(bf16[1040,128]{1,0:T(8,128)(2,1)S(1)} %other_kv.1.pay), channel_id=1, source_target_pairs={{0,2},{2,4},{4,6},{6,8},{8,10},{10,12},{12,14},{14,16},{16,18},{18... | collective-permute-start | bytes 798728 | tf_op jit(solution)/shard_map/ppermute | solution.py:213
  17.2 1.3 %collective-permute-start.2 = (bf16[1040,128]{1,0:T(8,128)(2,1)S(1)}, bf16[1040,128]{1,0:T(8,128)(2,1)S(1)}, u32[]{:S(2)}, u32[]{:S(2)}) collective-permute-start(bf16[1040,128]{1,0:T(8,128)(2,1)S(1)} %other_kv.1.pay), channel_id=1, source_target_pairs={{0,4},{2,6},{4,8},{6,10},{8,12},{10,14},{12,16},{14,18},{16,20},{1... | collective-permute-start | bytes 798728 | tf_op jit(solution)/shard_map/ppermute | solution.py:214
  18.6 0.0 copy-done
  18.6 2.4 %query.1 = (bf16[1024,128]{1,0:T(8,128)(2,1)S(1)}, bf16[2064,128]{1,0:T(8,128)(2,1)S(1)}) custom-call(bf16[128,4096]{1,0:T(8,128)(2,1)S(1)} %copy-done.3, bf16[128,4096]{1,0:T(8,128)(2,1)S(1)} %collective-permute-done.other, bf16[4096,1024]{1,0:T(8,128)(2,1)S(1)} %copy-done, bf16[1040,128]{1,0:T(8,128)(2,1)S(1)} %other_kv.1.pay), custom_call_target="tpu_custom_call" | custom-call | flops 2147483648 | bytes 11534336 | tf_op jit(solution)/shard_map/query/pallas_call | solution.py:215
  21.0 2.3 %collective-permute-start.1 = (bf16[2064,128]{1,0:T(8,128)(2,1)S(1)}, bf16[2064,128]{1,0:T(8,128)(2,1)S(1)}, u32[]{:S(2)}, u32[]{:S(2)}) collective-permute-start(bf16[2064,128]{1,0:T(8,128)(2,1)S(1)} %get-tuple-element.11), channel_id=1, source_target_pairs={{0,1},{1,0},{2,3},{3,2},{4,5},{5,4},{6,7},{7,6},{8,9},{9,8},{10,11... | collective-permute-start | bytes 1585160 | tf_op jit(solution)/shard_map/ppermute | solution.py:195
  23.3 0.0 collective-permute-done.4.near_mine
  23.3 2.9 %collective-permute-start.5 = (bf16[1040,128]{1,0:T(8,128)(2,1)S(1)}, bf16[1040,128]{1,0:T(8,128)(2,1)S(1)}, u32[]{:S(2)}, u32[]{:S(2)}) collective-permute-start(bf16[1040,128]{1,0:T(8,128)(2,1)S(1)} %collective-permute-done.4.near_mine), channel_id=1, source_target_pairs={{0,1},{1,0},{2,3},{3,2},{4,5},{5,4},{6,7},{7,6},{8,9},{9,8},{10,11... | collective-permute-start | bytes 798728 | tf_op jit(solution)/shard_map/ppermute | solution.py:195
  26.2 2.4 %collective-permute-done.2.far_mine = bf16[1040,128]{1,0:T(8,128)(2,1)S(1)} collective-permute-done((bf16[1040,128]{1,0:T(8,128)(2,1)S(1)}, bf16[1040,128]{1,0:T(8,128)(2,1)S(1)}, u32[]{:S(2)}, u32[]{:S(2)}) %collective-permute-start.2) | collective-permute-done | bytes 266272 | tf_op jit(solution)/shard_map/ppermute | solution.py:214
  28.6 2.8 %collective-permute-start.3 = (bf16[1040,128]{1,0:T(8,128)(2,1)S(1)}, bf16[1040,128]{1,0:T(8,128)(2,1)S(1)}, u32[]{:S(2)}, u32[]{:S(2)}) collective-permute-start(bf16[1040,128]{1,0:T(8,128)(2,1)S(1)} %collective-permute-done.2.far_mine), channel_id=1, source_target_pairs={{0,1},{1,0},{2,3},{3,2},{4,5},{5,4},{6,7},{7,6},{8,9},{9,8},{10,11... | collective-permute-start | bytes 798728 | tf_op jit(solution)/shard_map/ppermute | solution.py:195
  31.4 0.0 collective-permute-done.1.q_sent
  31.4 0.0 collective-permute-done.5.near_sent
  31.4 1.7 %attend_near.1 = (f32[2048,128]{1,0:T(8,128)S(1)}, f32[2048,128]{1,0:T(8,128)S(1)}, f32[2048,128]{1,0:T(8,128)S(1)}) custom-call(bf16[1024,128]{1,0:T(8,128)(2,1)S(1)} %get-tuple-element.10.q_mine, bf16[2064,128]{1,0:T(8,128)(2,1)S(1)} %collective-permute-done.1.q_sent, bf16[1040,128]{1,0:T(8,128)(2,1)S(1)} %other_kv.1.pay, ...), custom_call_target="tpu_custom_call" | custom-call | flops 1 | bytes 1 | tf_op jit(solution)/shard_map/attend_near/pallas_call | solution.py:228
  33.1 0.0 collective-permute-done.3.far_sent
  33.1 1.8 %attend_far.1 = bf16[128,2048]{1,0:T(8,128)(2,1)} custom-call(bf16[1024,128]{1,0:T(8,128)(2,1)S(1)} %get-tuple-element.10.q_mine, bf16[2064,128]{1,0:T(8,128)(2,1)S(1)} %collective-permute-done.1.q_sent, bf16[1040,128]{1,0:T(8,128)(2,1)S(1)} %other_kv.1.pay, bf16[1040,128]{1,0:T(8,128)(2,1)S(1)} %collective-permute-done.2.far_mine, ...), custom_call_target="tpu_custom_call" | custom-call | flops 268435456 | bytes 4194304 | tf_op jit(solution)/shard_map/attend_far/pallas_call | solution.py:237
  (4 shorter events, 0.0 us)
Async XLA Ops:
  0.0 12.7 %copy-start.3 = (bf16[128,4096]{1,0:T(8,128)(2,1)S(1)}, bf16[128,4096]{1,0:T(8,128)(2,1)}, u32[]{:S(2)}) copy-start(bf16[128,4096]{1,0:T(8,128)(2,1)} %own.3) | copy-start | bytes 3145732
  0.0 12.7 %copy-start.4 = (s32[128]{0:T(128)S(1)}, s32[128]{0:T(128)}, u32[]{:S(2)}) copy-start(s32[128]{0:T(128)} %param.6) | copy-start | bytes 1540
  0.0 12.7 %copy-start.1 = (bf16[4096,256]{1,0:T(8,128)(2,1)S(1)}, bf16[4096,256]{1,0:T(8,128)(2,1)}, u32[]{:S(2)}) copy-start(bf16[4096,256]{1,0:T(8,128)(2,1)} %ks.1) | copy-start | bytes 6291460
  0.0 12.7 %copy-start.2 = (bf16[4096,256]{1,0:T(8,128)(2,1)S(1)}, bf16[4096,256]{1,0:T(8,128)(2,1)}, u32[]{:S(2)}) copy-start(bf16[4096,256]{1,0:T(8,128)(2,1)} %vs.1) | copy-start | bytes 6291460
  0.0 15.2 %collective-permute-start = (bf16[128,4096]{1,0:T(8,128)(2,1)}, bf16[128,4096]{1,0:T(8,128)(2,1)S(1)}, u32[]{:S(2)}, u32[]{:S(2)}) collective-permute-start(bf16[128,4096]{1,0:T(8,128)(2,1)} %own.3), channel_id=1, source_target_pairs={{0,1},{1,0},{2,3},{3,2},{4,5},{5,4},{6,7},{7,6},{8,9},{9,8},{10,11... | collective-permute-start | bytes 3145736 | tf_op jit(solution)/shard_map/ppermute | solution.py:195
  12.7 5.8 %copy-start = (bf16[4096,1024]{1,0:T(8,128)(2,1)S(1)}, bf16[4096,1024]{1,0:T(8,128)(2,1)}, u32[]{:S(2)}) copy-start(bf16[4096,1024]{1,0:T(8,128)(2,1)} %w_query.1) | copy-start | bytes 25165828
  15.9 7.4 %collective-permute-start.4 = (bf16[1040,128]{1,0:T(8,128)(2,1)S(1)}, bf16[1040,128]{1,0:T(8,128)(2,1)S(1)}, u32[]{:S(2)}, u32[]{:S(2)}) collective-permute-start(bf16[1040,128]{1,0:T(8,128)(2,1)S(1)} %other_kv.1.pay), channel_id=1, source_target_pairs={{0,2},{2,4},{4,6},{6,8},{8,10},{10,12},{12,14},{14,16},{16,18},{18... | collective-permute-start | bytes 798728 | tf_op jit(solution)/shard_map/ppermute | solution.py:213
  17.2 11.4 %collective-permute-start.2 = (bf16[1040,128]{1,0:T(8,128)(2,1)S(1)}, bf16[1040,128]{1,0:T(8,128)(2,1)S(1)}, u32[]{:S(2)}, u32[]{:S(2)}) collective-permute-start(bf16[1040,128]{1,0:T(8,128)(2,1)S(1)} %other_kv.1.pay), channel_id=1, source_target_pairs={{0,4},{2,6},{4,8},{6,10},{8,12},{10,14},{12,16},{14,18},{16,20},{1... | collective-permute-start | bytes 798728 | tf_op jit(solution)/shard_map/ppermute | solution.py:214
  21.0 10.4 %collective-permute-start.1 = (bf16[2064,128]{1,0:T(8,128)(2,1)S(1)}, bf16[2064,128]{1,0:T(8,128)(2,1)S(1)}, u32[]{:S(2)}, u32[]{:S(2)}) collective-permute-start(bf16[2064,128]{1,0:T(8,128)(2,1)S(1)} %get-tuple-element.11), channel_id=1, source_target_pairs={{0,1},{1,0},{2,3},{3,2},{4,5},{5,4},{6,7},{7,6},{8,9},{9,8},{10,11... | collective-permute-start | bytes 1585160 | tf_op jit(solution)/shard_map/ppermute | solution.py:195
  23.3 8.1 %collective-permute-start.5 = (bf16[1040,128]{1,0:T(8,128)(2,1)S(1)}, bf16[1040,128]{1,0:T(8,128)(2,1)S(1)}, u32[]{:S(2)}, u32[]{:S(2)}) collective-permute-start(bf16[1040,128]{1,0:T(8,128)(2,1)S(1)} %collective-permute-done.4.near_mine), channel_id=1, source_target_pairs={{0,1},{1,0},{2,3},{3,2},{4,5},{5,4},{6,7},{7,6},{8,9},{9,8},{10,11... | collective-permute-start | bytes 798728 | tf_op jit(solution)/shard_map/ppermute | solution.py:195
  28.6 4.5 %collective-permute-start.3 = (bf16[1040,128]{1,0:T(8,128)(2,1)S(1)}, bf16[1040,128]{1,0:T(8,128)(2,1)S(1)}, u32[]{:S(2)}, u32[]{:S(2)}) collective-permute-start(bf16[1040,128]{1,0:T(8,128)(2,1)S(1)} %collective-permute-done.2.far_mine), channel_id=1, source_target_pairs={{0,1},{1,0},{2,3},{3,2},{4,5},{5,4},{6,7},{7,6},{8,9},{9,8},{10,11... | collective-permute-start | bytes 798728 | tf_op jit(solution)/shard_map/ppermute | solution.py:195

commit v3 on v2

--- a/solution.py
+++ b/solution.py
@@ -95,7 +95,26 @@
     return jnp.broadcast_to(x, (SHARE * ROWS, HEAD_SIZE))
 
 
-def near_kernel(q_mine, q_sent, pay, near_mine, near_sent, acc_out, m_out, l_out):
+def place(o, side, j, buf):
+    for i in range(SHARE):
+        col = (j * SHARE + i) * HEAD_SIZE
+        buf[side, :, col : col + HEAD_SIZE] = o[i * ROWS : (i + 1) * ROWS, :]
+
+
+def side_copy(buf, out, sem, side, j):
+    width = SHARE * HEAD_SIZE
+    start = jnp.where(lax.axis_index("head") == side, 0, HEADS * HEAD_SIZE) + j * width
+    to = out.at[:, pl.ds(pl.multiple_of(start, width), width)]
+    return pltpu.make_async_copy(buf.at[side, :, pl.ds(j * width, width)], to, sem.at[side, j])
+
+
+def wait_all(buf, out, sem):
+    for side in range(2):
+        for j in range(KV_HEADS):
+            side_copy(buf, out, sem, side, j).wait()
+
+
+def near_kernel(q_mine, q_sent, pay, near_mine, near_sent, out, acc_out, m_out, l_out, buf, sem):
     half = lax.axis_index("head")
     docs = ids_of(pay)
     doc_q = down(docs)
@@ -122,43 +141,46 @@
             top = jnp.max(s, axis=1, keepdims=True)
             p = jnp.exp2(s - top)
             to = pl.ds((side * HEADS + j * SHARE) * ROWS, SHARE * ROWS)
+            total = jnp.sum(p, axis=1, keepdims=True)
+            acc = dot(p.astype(BF16), v)
             m_out[to, :] = wide(top)
-            l_out[to, :] = wide(jnp.sum(p, axis=1, keepdims=True))
-            acc_out[to, :] = dot(p.astype(BF16), v)
-
-
-def far_kernel(q_mine, q_sent, pay, far_mine, far_sent, acc_in, m_in, l_in, out, buf, sem):
+            l_out[to, :] = wide(total)
+            acc_out[to, :] = acc
+            place((acc / total).astype(BF16), side, j, buf)
+            side_copy(buf, out, sem, side, j).start()
+    wait_all(buf, out, sem)
+
+
+def far_kernel(q_mine, q_sent, pay, far_mine, far_sent, acc_in, m_in, l_in, before, out, buf, sem):
     half = lax.axis_index("head")
-    doc_q = down(ids_of(pay))
-    far_a = jnp.where(doc_q == ids_of(far_mine), 0.0, NEG)
-    far_b = jnp.where(doc_q == ids_of(far_sent), 0.0, NEG)
-    copies = []
-    for side in range(2):
-        q_ref = (q_mine, q_sent)[side]
-        far = (far_mine, far_sent)[side]
-        bias = tall(far_a, far_b) if side == 0 else tall(far_b, far_a)
-        for j in range(KV_HEADS):
-            rows = pl.ds(j * SHARE * ROWS, SHARE * ROWS)
-            at = pl.ds((side * HEADS + j * SHARE) * ROWS, SHARE * ROWS)
-            s = dot_t(q_ref[rows, :], far[pl.ds(j * GROUP, GROUP), :]) * SCALE + bias
-            old = m_in[at, :]
-            top = jnp.maximum(old, wide(jnp.max(s, axis=1, keepdims=True)))
-            factor = jnp.exp2(old - top)
-            p = jnp.exp2(s - jnp.concatenate([top, top], axis=1))
-            total = l_in[at, :] * factor + wide(jnp.sum(p, axis=1, keepdims=True))
-            acc = acc_in[at, :] * factor
-            acc += dot(p.astype(BF16), far[pl.ds((KV_HEADS + j) * GROUP, GROUP), :])
-            o = (acc / total).astype(BF16)
-            for i in range(SHARE):
-                col = (j * SHARE + i) * HEAD_SIZE
-                buf[side, :, col : col + HEAD_SIZE] = o[i * ROWS : (i + 1) * ROWS, :]
-        width = HEADS * HEAD_SIZE
-        start = pl.multiple_of(jnp.where(half == side, 0, width), width)
-        copy = pltpu.make_async_copy(buf.at[side], out.at[:, pl.ds(start, width)], sem.at[side])
-        copy.start()
-        copies.append(copy)
-    for copy in copies:
-        copy.wait()
+    docs = ids_of(pay)
+    docs_a = ids_of(far_mine)
+    docs_b = ids_of(far_sent)
+    last = jnp.max(jnp.where(half == 0, docs_b, docs_a))
+
+    @pl.when(last == jnp.min(docs))
+    def _():
+        doc_q = down(docs)
+        far_a = jnp.where(doc_q == docs_a, 0.0, NEG)
+        far_b = jnp.where(doc_q == docs_b, 0.0, NEG)
+        for side in range(2):
+            q_ref = (q_mine, q_sent)[side]
+            far = (far_mine, far_sent)[side]
+            bias = tall(far_a, far_b) if side == 0 else tall(far_b, far_a)
+            for j in range(KV_HEADS):
+                rows = pl.ds(j * SHARE * ROWS, SHARE * ROWS)
+                at = pl.ds((side * HEADS + j * SHARE) * ROWS, SHARE * ROWS)
+                s = dot_t(q_ref[rows, :], far[pl.ds(j * GROUP, GROUP), :]) * SCALE + bias
+                old = m_in[at, :]
+                top = jnp.maximum(old, wide(jnp.max(s, axis=1, keepdims=True)))
+                factor = jnp.exp2(old - top)
+                p = jnp.exp2(s - jnp.concatenate([top, top], axis=1))
+                total = l_in[at, :] * factor + wide(jnp.sum(p, axis=1, keepdims=True))
+                acc = acc_in[at, :] * factor
+                acc += dot(p.astype(BF16), far[pl.ds((KV_HEADS + j) * GROUP, GROUP), :])
+                place((acc / total).astype(BF16), side, j, buf)
+                side_copy(buf, out, sem, side, j).start()
+        wait_all(buf, out, sem)
 
 
 VMEM = pl.BlockSpec(memory_space=pltpu.VMEM)
@@ -166,13 +188,14 @@
 DMA = pltpu.SemaphoreType.DMA
 
 
-def call(kernel, name, outs, ins, mib, flops, size, scratch=(), to=None):
+def call(kernel, name, outs, ins, mib, flops, size, scratch=(), to=None, alias={}):
     many = isinstance(outs, list)
     return pl.pallas_call(
         kernel,
         out_shape=outs,
         in_specs=ins,
-        out_specs=[VMEM] * len(outs) if many else to or VMEM,
+        out_specs=to or ([VMEM] * len(outs) if many else VMEM),
+        input_output_aliases=alias,
         scratch_shapes=list(scratch),
         compiler_params=pltpu.CompilerParams(vmem_limit_bytes=mib << 20),
         cost_estimate=pl.CostEstimate(flops=flops, bytes_accessed=size, transcendentals=0),
@@ -225,26 +248,31 @@
     near_sent = swap(near)
     far_sent = swap(far)
     pairs = ROWS * GROUP * 2 * HEADS * HEAD_SIZE
-    acc, m, l = call(
+    result = jax.ShapeDtypeStruct((ROWS, 2 * HEADS * HEAD_SIZE), BF16)
+    sides = [pltpu.VMEM((2, ROWS, HEADS * HEAD_SIZE), BF16), DMA((2, KV_HEADS))]
+    out, acc, m, l = call(
         near_kernel,
         "attend_near",
-        [pltpu.VMEM((2 * Q_ROWS, n), F32) for n in [HEAD_SIZE] * 3],
+        [result] + [pltpu.VMEM((2 * Q_ROWS, HEAD_SIZE), F32)] * 3,
         [VMEM] * 5,
         16,
         1,
         1,
+        sides,
+        [ANY] + [VMEM] * 3,
     )(q_mine, q_sent, pay, near, near_sent)
     return call(
         far_kernel,
         "attend_far",
-        jax.ShapeDtypeStruct((ROWS, 2 * HEADS * HEAD_SIZE), BF16),
-        [VMEM] * 8,
+        result,
+        [VMEM] * 8 + [ANY],
         16,
         4 * pairs,
         4 << 20,
-        [pltpu.VMEM((2, ROWS, HEADS * HEAD_SIZE), BF16), DMA((2,))],
+        sides,
         ANY,
-    )(q_mine, q_sent, pay, far, far_sent, acc, m, l)
+        {8: 0},
+    )(q_mine, q_sent, pay, far, far_sent, acc, m, l, out)
 
 
 def solution(mesh):

time: 35.4 us -> 34.4 us (0.972)
  Pallas kernels: 7.39 us -> 6.49 us
    pallas_call x2, Pallas kernels: 3.48 us -> 2.57 us  [the longest x1 2.4 us: on_device(): call(near_kernel, 'attend_near', [result] + [pltpu.VMEM((2 * Q_ROWS, HEAD...]
  transfers between devices with their start and end apart: 6 -> 6, of which waited for: 2 -> 2; matrix products, arithmetic and copies ran while one was open for 0% -> 0% of each run, Pallas kernels for 14% -> 16%
where the time goes in v3:
time: 34.4 us; the launch traced here: 34 us
  starting transfers between devices  23.2 us (67%)
  Pallas kernels  6.49 us (19%)
  waiting for transfers between devices  4.1 us (12%)
    ppermute x4, starting transfers between devices, swap(): return lax.ppermute(x, 'head', [(0, 1), (1, 0)])  20.6 us
    pallas_call x1, Pallas kernels, on_device(): call(query_kernel, 'query', [bf16(Q_ROWS, HEAD_SIZE), bf16(Q_ROWS + PAY_R...  2.43 us
    ppermute x1, waiting for transfers between devices, on_device(): far = lax.ppermute(pay, 'srv', [(i, i + 2) for i in range(groups - 2)])  2.42 us
    pallas_call x1, Pallas kernels, on_device(): call(near_kernel, 'attend_near', [result] + [pltpu.VMEM((2 * Q_ROWS, HEAD...  2.4 us
    ppermute x4, waiting for transfers between devices, swap(): return lax.ppermute(x, 'head', [(0, 1), (1, 0)])  1.67 us
    ppermute x1, starting transfers between devices, on_device(): far = lax.ppermute(pay, 'srv', [(i, i + 2) for i in range(groups - 2)])  1.31 us
    ppermute x1, starting transfers between devices, on_device(): near = lax.ppermute(pay, 'srv', [(i, i + 1) for i in range(groups - 1)])  1.31 us
    pallas_call x1, Pallas kernels, on_device(): call(own_kv_kernel, 'own_kv', bf16(2 * KV_HEADS * ROWS + DOC_ROWS, HEAD_S...  0.75 us
  transfers between devices with their start and end apart: 6, of which 2 were waited for; matrix products, arithmetic and copies ran while one was open for 0% of the time, Pallas kernels for 16%

profile of v3, /device:TPU:1, one launch (start us, length us, event | category | flops | bytes accessed | tf_op | source)
XLA Modules:
  0.0 34.0 jit_solution(14845994578378101976)
XLA Ops:
  0.0 0.0 copy-start.2
  0.0 12.7 %collective-permute-start = (bf16[128,4096]{1,0:T(8,128)(2,1)}, bf16[128,4096]{1,0:T(8,128)(2,1)S(1)}, u32[]{:S(2)}, u32[]{:S(2)}) collective-permute-start(bf16[128,4096]{1,0:T(8,128)(2,1)} %own.3), channel_id=1, source_target_pairs={{0,1},{1,0},{2,3},{3,2},{4,5},{5,4},{6,7},{7,6},{8,9},{9,8},{10,11... | collective-permute-start | bytes 3145736 | tf_op jit(solution)/shard_map/ppermute | solution.py:218
  12.7 0.0 copy-done.3
  12.7 0.0 copy-done.4
  12.7 0.0 copy-done.1
  12.7 0.0 copy-done.2
  12.7 0.0 copy-start
  12.8 0.7 %own_kv.1.own_pay = bf16[528,128]{1,0:T(8,128)(2,1)S(1)} custom-call(bf16[16,128]{1,0:T(8,128)(2,1)S(1)} %first.1, bf16[128,4096]{1,0:T(8,128)(2,1)S(1)} %copy-done.3, bf16[4096,256]{1,0:T(8,128)(2,1)S(1)} %copy-done.1, bf16[4096,256]{1,0:T(8,128)(2,1)S(1)} %copy-done.2, s32[1,128]{1,0:T(1,128)S(1)} %bitcast.1), custom_call_target="tpu_custom_call" | custom-call | flops 536870912 | bytes 5242880 | tf_op jit(solution)/shard_map/own_kv/pallas_call | solution.py:224
  13.5 1.7 %collective-permute-done.other = bf16[128,4096]{1,0:T(8,128)(2,1)S(1)} collective-permute-done((bf16[128,4096]{1,0:T(8,128)(2,1)}, bf16[128,4096]{1,0:T(8,128)(2,1)S(1)}, u32[]{:S(2)}, u32[]{:S(2)}) %collective-permute-start) | collective-permute-done | bytes 1048608 | tf_op jit(solution)/shard_map/ppermute | solution.py:218
  15.2 0.7 %other_kv.1.pay = bf16[1040,128]{1,0:T(8,128)(2,1)S(1)} custom-call(bf16[128,4096]{1,0:T(8,128)(2,1)S(1)} %collective-permute-done.other, bf16[528,128]{1,0:T(8,128)(2,1)S(1)} %own_kv.1.own_pay, bf16[4096,256]{1,0:T(8,128)(2,1)S(1)} %copy-done.1, bf16[4096,256]{1,0:T(8,128)(2,1)S(1)} %copy-done.2), custom_call_target="tpu_custom_call" | custom-call | flops 536870912 | bytes 5242880 | tf_op jit(solution)/shard_map/other_kv/pallas_call | solution.py:233
  15.9 1.3 %collective-permute-start.4 = (bf16[1040,128]{1,0:T(8,128)(2,1)S(1)}, bf16[1040,128]{1,0:T(8,128)(2,1)S(1)}, u32[]{:S(2)}, u32[]{:S(2)}) collective-permute-start(bf16[1040,128]{1,0:T(8,128)(2,1)S(1)} %other_kv.1.pay), channel_id=1, source_target_pairs={{0,2},{2,4},{4,6},{6,8},{8,10},{10,12},{12,14},{14,16},{16,18},{18... | collective-permute-start | bytes 798728 | tf_op jit(solution)/shard_map/ppermute | solution.py:236
  17.2 1.3 %collective-permute-start.2 = (bf16[1040,128]{1,0:T(8,128)(2,1)S(1)}, bf16[1040,128]{1,0:T(8,128)(2,1)S(1)}, u32[]{:S(2)}, u32[]{:S(2)}) collective-permute-start(bf16[1040,128]{1,0:T(8,128)(2,1)S(1)} %other_kv.1.pay), channel_id=1, source_target_pairs={{0,4},{2,6},{4,8},{6,10},{8,12},{10,14},{12,16},{14,18},{16,20},{1... | collective-permute-start | bytes 798728 | tf_op jit(solution)/shard_map/ppermute | solution.py:237
  18.6 0.0 copy-done
  18.6 2.4 %query.1 = (bf16[1024,128]{1,0:T(8,128)(2,1)S(1)}, bf16[2064,128]{1,0:T(8,128)(2,1)S(1)}) custom-call(bf16[128,4096]{1,0:T(8,128)(2,1)S(1)} %copy-done.3, bf16[128,4096]{1,0:T(8,128)(2,1)S(1)} %collective-permute-done.other, bf16[4096,1024]{1,0:T(8,128)(2,1)S(1)} %copy-done, bf16[1040,128]{1,0:T(8,128)(2,1)S(1)} %other_kv.1.pay), custom_call_target="tpu_custom_call" | custom-call | flops 2147483648 | bytes 11534336 | tf_op jit(solution)/shard_map/query/pallas_call | solution.py:238
  21.0 2.3 %collective-permute-start.1 = (bf16[2064,128]{1,0:T(8,128)(2,1)S(1)}, bf16[2064,128]{1,0:T(8,128)(2,1)S(1)}, u32[]{:S(2)}, u32[]{:S(2)}) collective-permute-start(bf16[2064,128]{1,0:T(8,128)(2,1)S(1)} %get-tuple-element.12), channel_id=1, source_target_pairs={{0,1},{1,0},{2,3},{3,2},{4,5},{5,4},{6,7},{7,6},{8,9},{9,8},{10,11... | collective-permute-start | bytes 1585160 | tf_op jit(solution)/shard_map/ppermute | solution.py:218
  23.3 0.0 collective-permute-done.4.near_mine
  23.3 2.9 %collective-permute-start.5 = (bf16[1040,128]{1,0:T(8,128)(2,1)S(1)}, bf16[1040,128]{1,0:T(8,128)(2,1)S(1)}, u32[]{:S(2)}, u32[]{:S(2)}) collective-permute-start(bf16[1040,128]{1,0:T(8,128)(2,1)S(1)} %collective-permute-done.4.near_mine), channel_id=1, source_target_pairs={{0,1},{1,0},{2,3},{3,2},{4,5},{5,4},{6,7},{7,6},{8,9},{9,8},{10,11... | collective-permute-start | bytes 798728 | tf_op jit(solution)/shard_map/ppermute | solution.py:218
  26.2 2.4 %collective-permute-done.2.far_mine = bf16[1040,128]{1,0:T(8,128)(2,1)S(1)} collective-permute-done((bf16[1040,128]{1,0:T(8,128)(2,1)S(1)}, bf16[1040,128]{1,0:T(8,128)(2,1)S(1)}, u32[]{:S(2)}, u32[]{:S(2)}) %collective-permute-start.2) | collective-permute-done | bytes 266272 | tf_op jit(solution)/shard_map/ppermute | solution.py:237
  28.6 2.8 %collective-permute-start.3 = (bf16[1040,128]{1,0:T(8,128)(2,1)S(1)}, bf16[1040,128]{1,0:T(8,128)(2,1)S(1)}, u32[]{:S(2)}, u32[]{:S(2)}) collective-permute-start(bf16[1040,128]{1,0:T(8,128)(2,1)S(1)} %collective-permute-done.2.far_mine), channel_id=1, source_target_pairs={{0,1},{1,0},{2,3},{3,2},{4,5},{5,4},{6,7},{7,6},{8,9},{9,8},{10,11... | collective-permute-start | bytes 798728 | tf_op jit(solution)/shard_map/ppermute | solution.py:218
  31.4 0.0 collective-permute-done.1.q_sent
  31.4 0.0 collective-permute-done.5.near_sent
  31.4 2.4 %attend_near.1 = (bf16[128,2048]{1,0:T(8,128)(2,1)}, f32[2048,128]{1,0:T(8,128)S(1)}, f32[2048,128]{1,0:T(8,128)S(1)}, f32[2048,128]{1,0:T(8,128)S(1)}) custom-call(bf16[1024,128]{1,0:T(8,128)(2,1)S(1)} %get-tuple-element.11.q_mine, bf16[2064,128]{1,0:T(8,128)(2,1)S(1)} %collective-permute-done.1.q_sent, bf16[1040,128]{1,0:T(8,128)(2,1)S(1)} %other_kv.1.pay, ...), custom_call_target="tpu_custom_call" | custom-call | flops 1 | bytes 1 | tf_op jit(solution)/shard_map/attend_near/pallas_call | solution.py:253
  33.8 0.0 collective-permute-done.3.far_sent
  33.9 0.2 attend_far.1
  (4 shorter events, 0.0 us)
Async XLA Ops:
  0.0 12.7 %copy-start.3 = (bf16[128,4096]{1,0:T(8,128)(2,1)S(1)}, bf16[128,4096]{1,0:T(8,128)(2,1)}, u32[]{:S(2)}) copy-start(bf16[128,4096]{1,0:T(8,128)(2,1)} %own.3) | copy-start | bytes 3145732
  0.0 12.7 %copy-start.4 = (s32[128]{0:T(128)S(1)}, s32[128]{0:T(128)}, u32[]{:S(2)}) copy-start(s32[128]{0:T(128)} %param.6) | copy-start | bytes 1540
  0.0 12.7 %copy-start.1 = (bf16[4096,256]{1,0:T(8,128)(2,1)S(1)}, bf16[4096,256]{1,0:T(8,128)(2,1)}, u32[]{:S(2)}) copy-start(bf16[4096,256]{1,0:T(8,128)(2,1)} %ks.1) | copy-start | bytes 6291460
  0.0 12.7 %copy-start.2 = (bf16[4096,256]{1,0:T(8,128)(2,1)S(1)}, bf16[4096,256]{1,0:T(8,128)(2,1)}, u32[]{:S(2)}) copy-start(bf16[4096,256]{1,0:T(8,128)(2,1)} %vs.1) | copy-start | bytes 6291460
  0.0 15.2 %collective-permute-start = (bf16[128,4096]{1,0:T(8,128)(2,1)}, bf16[128,4096]{1,0:T(8,128)(2,1)S(1)}, u32[]{:S(2)}, u32[]{:S(2)}) collective-permute-start(bf16[128,4096]{1,0:T(8,128)(2,1)} %own.3), channel_id=1, source_target_pairs={{0,1},{1,0},{2,3},{3,2},{4,5},{5,4},{6,7},{7,6},{8,9},{9,8},{10,11... | collective-permute-start | bytes 3145736 | tf_op jit(solution)/shard_map/ppermute | solution.py:218
  12.7 5.8 %copy-start = (bf16[4096,1024]{1,0:T(8,128)(2,1)S(1)}, bf16[4096,1024]{1,0:T(8,128)(2,1)}, u32[]{:S(2)}) copy-start(bf16[4096,1024]{1,0:T(8,128)(2,1)} %w_query.1) | copy-start | bytes 25165828
  15.9 7.4 %collective-permute-start.4 = (bf16[1040,128]{1,0:T(8,128)(2,1)S(1)}, bf16[1040,128]{1,0:T(8,128)(2,1)S(1)}, u32[]{:S(2)}, u32[]{:S(2)}) collective-permute-start(bf16[1040,128]{1,0:T(8,128)(2,1)S(1)} %other_kv.1.pay), channel_id=1, source_target_pairs={{0,2},{2,4},{4,6},{6,8},{8,10},{10,12},{12,14},{14,16},{16,18},{18... | collective-permute-start | bytes 798728 | tf_op jit(solution)/shard_map/ppermute | solution.py:236
  17.2 11.4 %collective-permute-start.2 = (bf16[1040,128]{1,0:T(8,128)(2,1)S(1)}, bf16[1040,128]{1,0:T(8,128)(2,1)S(1)}, u32[]{:S(2)}, u32[]{:S(2)}) collective-permute-start(bf16[1040,128]{1,0:T(8,128)(2,1)S(1)} %other_kv.1.pay), channel_id=1, source_target_pairs={{0,4},{2,6},{4,8},{6,10},{8,12},{10,14},{12,16},{14,18},{16,20},{1... | collective-permute-start | bytes 798728 | tf_op jit(solution)/shard_map/ppermute | solution.py:237
  21.0 10.4 %collective-permute-start.1 = (bf16[2064,128]{1,0:T(8,128)(2,1)S(1)}, bf16[2064,128]{1,0:T(8,128)(2,1)S(1)}, u32[]{:S(2)}, u32[]{:S(2)}) collective-permute-start(bf16[2064,128]{1,0:T(8,128)(2,1)S(1)} %get-tuple-element.12), channel_id=1, source_target_pairs={{0,1},{1,0},{2,3},{3,2},{4,5},{5,4},{6,7},{7,6},{8,9},{9,8},{10,11... | collective-permute-start | bytes 1585160 | tf_op jit(solution)/shard_map/ppermute | solution.py:218
  23.3 8.1 %collective-permute-start.5 = (bf16[1040,128]{1,0:T(8,128)(2,1)S(1)}, bf16[1040,128]{1,0:T(8,128)(2,1)S(1)}, u32[]{:S(2)}, u32[]{:S(2)}) collective-permute-start(bf16[1040,128]{1,0:T(8,128)(2,1)S(1)} %collective-permute-done.4.near_mine), channel_id=1, source_target_pairs={{0,1},{1,0},{2,3},{3,2},{4,5},{5,4},{6,7},{7,6},{8,9},{9,8},{10,11... | collective-permute-start | bytes 798728 | tf_op jit(solution)/shard_map/ppermute | solution.py:218
  28.6 5.2 %collective-permute-start.3 = (bf16[1040,128]{1,0:T(8,128)(2,1)S(1)}, bf16[1040,128]{1,0:T(8,128)(2,1)S(1)}, u32[]{:S(2)}, u32[]{:S(2)}) collective-permute-start(bf16[1040,128]{1,0:T(8,128)(2,1)S(1)} %collective-permute-done.2.far_mine), channel_id=1, source_target_pairs={{0,1},{1,0},{2,3},{3,2},{4,5},{5,4},{6,7},{7,6},{8,9},{9,8},{10,11... | collective-permute-start | bytes 798728 | tf_op jit(solution)/shard_map/ppermute | solution.py:218

commit v4 on v3

--- a/solution.py
+++ b/solution.py
@@ -87,8 +87,13 @@
     return jnp.transpose(jnp.broadcast_to(ids, (ROWS, ROWS)))
 
 
-def tall(*blocks):
-    return jnp.concatenate([jnp.concatenate(blocks, axis=1)] * SHARE, axis=0)
+def scores(q, k, bias):
+    s = dot_t(q, k).reshape(SHARE, ROWS, k.shape[0]) * SCALE + bias[None]
+    return s.reshape(SHARE * ROWS, k.shape[0])
+
+
+def side_by_side(*blocks):
+    return jnp.concatenate(blocks, axis=1)
 
 
 def wide(x):
@@ -114,63 +119,75 @@
             side_copy(buf, out, sem, side, j).wait()
 
 
-def near_kernel(q_mine, q_sent, pay, near_mine, near_sent, out, acc_out, m_out, l_out, buf, sem):
+def near_kernel(q_mine, q_sent, pay, near_mine, near_sent, out, acc_out, m_out, l_out, flag, buf, sem):
     half = lax.axis_index("head")
     docs = ids_of(pay)
     doc_q = down(docs)
     r = lax.broadcasted_iota(jnp.int32, (ROWS, ROWS), 0)
     c = lax.broadcasted_iota(jnp.int32, (ROWS, ROWS), 1)
-    here_mine = jnp.where((doc_q == docs) & (c <= r), 0.0, NEG)
-    here_other = jnp.where((doc_q == ids_of(q_sent, Q_ROWS)) & (c < half * ROWS), 0.0, NEG)
+    here_a = jnp.where((doc_q == docs) & (c <= r), 0.0, NEG)
+    here_b = jnp.where((doc_q == ids_of(q_sent, Q_ROWS)) & (c < half * ROWS), 0.0, NEG)
     near_a = jnp.where(doc_q == ids_of(near_mine), 0.0, NEG)
     near_b = jnp.where(doc_q == ids_of(near_sent), 0.0, NEG)
-    for side in range(2):
-        if side == 0:
-            q_ref, here, start, near = q_mine, pay, 0, near_mine
-            bias = tall(here_mine, here_other, near_a, near_b)
-        else:
-            q_ref, here, start, near = q_sent, q_sent, Q_ROWS, near_sent
-            bias = tall(here_other, here_mine, near_b, near_a)
-        for j in range(KV_HEADS):
-            rows = pl.ds(j * SHARE * ROWS, SHARE * ROWS)
-            k_at = j * GROUP
-            v_at = (KV_HEADS + j) * GROUP
-            k = jnp.concatenate([here[pl.ds(start + k_at, GROUP), :], near[pl.ds(k_at, GROUP), :]], axis=0)
-            v = jnp.concatenate([here[pl.ds(start + v_at, GROUP), :], near[pl.ds(v_at, GROUP), :]], axis=0)
-            s = dot_t(q_ref[rows, :], k) * SCALE + bias
-            top = jnp.max(s, axis=1, keepdims=True)
-            p = jnp.exp2(s - top)
-            to = pl.ds((side * HEADS + j * SHARE) * ROWS, SHARE * ROWS)
-            total = jnp.sum(p, axis=1, keepdims=True)
-            acc = dot(p.astype(BF16), v)
-            m_out[to, :] = wide(top)
-            l_out[to, :] = wide(total)
-            acc_out[to, :] = acc
-            place((acc / total).astype(BF16), side, j, buf)
-            side_copy(buf, out, sem, side, j).start()
-    wait_all(buf, out, sem)
-
-
-def far_kernel(q_mine, q_sent, pay, far_mine, far_sent, acc_in, m_in, l_in, before, out, buf, sem):
-    half = lax.axis_index("head")
-    docs = ids_of(pay)
-    docs_a = ids_of(far_mine)
-    docs_b = ids_of(far_sent)
-    last = jnp.max(jnp.where(half == 0, docs_b, docs_a))
-
-    @pl.when(last == jnp.min(docs))
+
+    def attend(final):
+        for side in range(2):
+            if side == 0:
+                q_ref, here, start, near = q_mine, pay, 0, near_mine
+                bias = side_by_side(here_a, here_b, near_a, near_b)
+            else:
+                q_ref, here, start, near = q_sent, q_sent, Q_ROWS, near_sent
+                bias = side_by_side(here_b, here_a, near_b, near_a)
+
+            def gather(j):
+                at = j * GROUP
+                return jnp.concatenate([here[pl.ds(start + at, GROUP), :], near[pl.ds(at, GROUP), :]], axis=0)
+
+            for j in range(KV_HEADS):
+                rows = pl.ds(j * SHARE * ROWS, SHARE * ROWS)
+                s = scores(q_ref[rows, :], gather(j), bias)
+                top = jnp.max(s, axis=1, keepdims=True)
+                p = jnp.exp2(s - top)
+                total = jnp.sum(p, axis=1, keepdims=True)
+                acc = dot(p.astype(BF16), gather(KV_HEADS + j))
+                if final:
+                    place((acc / total).astype(BF16), side, j, buf)
+                    side_copy(buf, out, sem, side, j).start()
+                else:
+                    to = pl.ds((side * HEADS + j * SHARE) * ROWS, SHARE * ROWS)
+                    m_out[to, :] = wide(top)
+                    l_out[to, :] = wide(total)
+                    acc_out[to, :] = acc
+        if final:
+            wait_all(buf, out, sem)
+
+    first = jnp.where(half == 0, ids_of(near_mine), ids_of(near_sent))
+    more = jnp.min(first) == jnp.min(docs)
+    flag[...] = jnp.where(more, 1.0, 0.0) * jnp.ones_like(flag)
+
+    @pl.when(more)
     def _():
-        doc_q = down(docs)
-        far_a = jnp.where(doc_q == docs_a, 0.0, NEG)
-        far_b = jnp.where(doc_q == docs_b, 0.0, NEG)
+        attend(False)
+
+    @pl.when(jnp.logical_not(more))
+    def _():
+        attend(True)
+
+
+def far_kernel(q_mine, q_sent, pay, far_mine, far_sent, acc_in, m_in, l_in, flag, before, out, buf, sem):
+    @pl.when(jnp.max(flag[...]) > 0.5)
+    def _():
+        doc_q = down(ids_of(pay))
+        far_a = jnp.where(doc_q == ids_of(far_mine), 0.0, NEG)
+        far_b = jnp.where(doc_q == ids_of(far_sent), 0.0, NEG)
         for side in range(2):
             q_ref = (q_mine, q_sent)[side]
             far = (far_mine, far_sent)[side]
-            bias = tall(far_a, far_b) if side == 0 else tall(far_b, far_a)
+            bias = side_by_side(far_a, far_b) if side == 0 else side_by_side(far_b, far_a)
             for j in range(KV_HEADS):
                 rows = pl.ds(j * SHARE * ROWS, SHARE * ROWS)
                 at = pl.ds((side * HEADS + j * SHARE) * ROWS, SHARE * ROWS)
-                s = dot_t(q_ref[rows, :], far[pl.ds(j * GROUP, GROUP), :]) * SCALE + bias
+                s = scores(q_ref[rows, :], far[pl.ds(j * GROUP, GROUP), :], bias)
                 old = m_in[at, :]
                 top = jnp.maximum(old, wide(jnp.max(s, axis=1, keepdims=True)))
                 factor = jnp.exp2(old - top)
@@ -250,29 +267,29 @@
     pairs = ROWS * GROUP * 2 * HEADS * HEAD_SIZE
     result = jax.ShapeDtypeStruct((ROWS, 2 * HEADS * HEAD_SIZE), BF16)
     sides = [pltpu.VMEM((2, ROWS, HEADS * HEAD_SIZE), BF16), DMA((2, KV_HEADS))]
-    out, acc, m, l = call(
+    out, acc, m, l, flag = call(
         near_kernel,
         "attend_near",
-        [result] + [pltpu.VMEM((2 * Q_ROWS, HEAD_SIZE), F32)] * 3,
+        [result] + [pltpu.VMEM((2 * Q_ROWS, HEAD_SIZE), F32)] * 3 + [pltpu.VMEM((8, HEAD_SIZE), F32)],
         [VMEM] * 5,
         16,
         1,
         1,
         sides,
-        [ANY] + [VMEM] * 3,
+        [ANY] + [VMEM] * 4,
     )(q_mine, q_sent, pay, near, near_sent)
     return call(
         far_kernel,
         "attend_far",
         result,
-        [VMEM] * 8 + [ANY],
+        [VMEM] * 9 + [ANY],
         16,
         4 * pairs,
         4 << 20,
         sides,
         ANY,
-        {8: 0},
-    )(q_mine, q_sent, pay, far, far_sent, acc, m, l, out)
+        {9: 0},
+    )(q_mine, q_sent, pay, far, far_sent, acc, m, l, flag, out)
 
 
 def solution(mesh):

time: 34.4 us -> 34.6 us (level)
  transfers between devices with their start and end apart: 6 -> 6, of which waited for: 2 -> 2; matrix products, arithmetic and copies ran while one was open for 0% -> 0% of each run, Pallas kernels for 16% -> 17%
where the time goes in v4:
time: 34.6 us; the launch traced here: 34.2 us
  starting transfers between devices  23.2 us (67%)
  Pallas kernels  6.62 us (19%)
  waiting for transfers between devices  4.1 us (12%)
    ppermute x4, starting transfers between devices, swap(): return lax.ppermute(x, 'head', [(0, 1), (1, 0)])  20.6 us
    pallas_call x1, Pallas kernels, on_device(): call(near_kernel, 'attend_near', [result] + [pltpu.VMEM((2 * Q_ROWS, HEAD...  2.54 us
    pallas_call x1, Pallas kernels, on_device(): call(query_kernel, 'query', [bf16(Q_ROWS, HEAD_SIZE), bf16(Q_ROWS + PAY_R...  2.43 us
    ppermute x1, waiting for transfers between devices, on_device(): far = lax.ppermute(pay, 'srv', [(i, i + 2) for i in range(groups - 2)])  2.42 us
    ppermute x4, waiting for transfers between devices, swap(): return lax.ppermute(x, 'head', [(0, 1), (1, 0)])  1.67 us
    ppermute x1, starting transfers between devices, on_device(): near = lax.ppermute(pay, 'srv', [(i, i + 1) for i in range(groups - 1)])  1.31 us
    ppermute x1, starting transfers between devices, on_device(): far = lax.ppermute(pay, 'srv', [(i, i + 2) for i in range(groups - 2)])  1.31 us
    pallas_call x1, Pallas kernels, on_device(): call(own_kv_kernel, 'own_kv', bf16(2 * KV_HEADS * ROWS + DOC_ROWS, HEAD_S...  0.75 us
  transfers between devices with their start and end apart: 6, of which 2 were waited for; matrix products, arithmetic and copies ran while one was open for 0% of the time, Pallas kernels for 17%

profile of v4, /device:TPU:1, one launch (start us, length us, event | category | flops | bytes accessed | tf_op | source)
XLA Modules:
  0.0 34.2 jit_solution(5728000073153815807)
XLA Ops:
  0.0 0.0 copy-start.2
  0.0 12.7 %collective-permute-start = (bf16[128,4096]{1,0:T(8,128)(2,1)}, bf16[128,4096]{1,0:T(8,128)(2,1)S(1)}, u32[]{:S(2)}, u32[]{:S(2)}) collective-permute-start(bf16[128,4096]{1,0:T(8,128)(2,1)} %own.3), channel_id=1, source_target_pairs={{0,1},{1,0},{2,3},{3,2},{4,5},{5,4},{6,7},{7,6},{8,9},{9,8},{10,11... | collective-permute-start | bytes 3145736 | tf_op jit(solution)/shard_map/ppermute | solution.py:235
  12.7 0.0 copy-done.3
  12.7 0.0 copy-done.4
  12.7 0.0 copy-done.1
  12.7 0.0 copy-done.2
  12.7 0.0 copy-start
  12.8 0.7 %own_kv.1.own_pay = bf16[528,128]{1,0:T(8,128)(2,1)S(1)} custom-call(bf16[16,128]{1,0:T(8,128)(2,1)S(1)} %first.1, bf16[128,4096]{1,0:T(8,128)(2,1)S(1)} %copy-done.3, bf16[4096,256]{1,0:T(8,128)(2,1)S(1)} %copy-done.1, bf16[4096,256]{1,0:T(8,128)(2,1)S(1)} %copy-done.2, s32[1,128]{1,0:T(1,128)S(1)} %bitcast.1), custom_call_target="tpu_custom_call" | custom-call | flops 536870912 | bytes 5242880 | tf_op jit(solution)/shard_map/own_kv/pallas_call | solution.py:241
  13.5 1.7 %collective-permute-done.other = bf16[128,4096]{1,0:T(8,128)(2,1)S(1)} collective-permute-done((bf16[128,4096]{1,0:T(8,128)(2,1)}, bf16[128,4096]{1,0:T(8,128)(2,1)S(1)}, u32[]{:S(2)}, u32[]{:S(2)}) %collective-permute-start) | collective-permute-done | bytes 1048608 | tf_op jit(solution)/shard_map/ppermute | solution.py:235
  15.2 0.7 %other_kv.1.pay = bf16[1040,128]{1,0:T(8,128)(2,1)S(1)} custom-call(bf16[128,4096]{1,0:T(8,128)(2,1)S(1)} %collective-permute-done.other, bf16[528,128]{1,0:T(8,128)(2,1)S(1)} %own_kv.1.own_pay, bf16[4096,256]{1,0:T(8,128)(2,1)S(1)} %copy-done.1, bf16[4096,256]{1,0:T(8,128)(2,1)S(1)} %copy-done.2), custom_call_target="tpu_custom_call" | custom-call | flops 536870912 | bytes 5242880 | tf_op jit(solution)/shard_map/other_kv/pallas_call | solution.py:250
  15.9 1.3 %collective-permute-start.4 = (bf16[1040,128]{1,0:T(8,128)(2,1)S(1)}, bf16[1040,128]{1,0:T(8,128)(2,1)S(1)}, u32[]{:S(2)}, u32[]{:S(2)}) collective-permute-start(bf16[1040,128]{1,0:T(8,128)(2,1)S(1)} %other_kv.1.pay), channel_id=1, source_target_pairs={{0,2},{2,4},{4,6},{6,8},{8,10},{10,12},{12,14},{14,16},{16,18},{18... | collective-permute-start | bytes 798728 | tf_op jit(solution)/shard_map/ppermute | solution.py:253
  17.2 1.3 %collective-permute-start.2 = (bf16[1040,128]{1,0:T(8,128)(2,1)S(1)}, bf16[1040,128]{1,0:T(8,128)(2,1)S(1)}, u32[]{:S(2)}, u32[]{:S(2)}) collective-permute-start(bf16[1040,128]{1,0:T(8,128)(2,1)S(1)} %other_kv.1.pay), channel_id=1, source_target_pairs={{0,4},{2,6},{4,8},{6,10},{8,12},{10,14},{12,16},{14,18},{16,20},{1... | collective-permute-start | bytes 798728 | tf_op jit(solution)/shard_map/ppermute | solution.py:254
  18.6 0.0 copy-done
  18.6 2.4 %query.1 = (bf16[1024,128]{1,0:T(8,128)(2,1)S(1)}, bf16[2064,128]{1,0:T(8,128)(2,1)S(1)}) custom-call(bf16[128,4096]{1,0:T(8,128)(2,1)S(1)} %copy-done.3, bf16[128,4096]{1,0:T(8,128)(2,1)S(1)} %collective-permute-done.other, bf16[4096,1024]{1,0:T(8,128)(2,1)S(1)} %copy-done, bf16[1040,128]{1,0:T(8,128)(2,1)S(1)} %other_kv.1.pay), custom_call_target="tpu_custom_call" | custom-call | flops 2147483648 | bytes 11534336 | tf_op jit(solution)/shard_map/query/pallas_call | solution.py:255
  21.0 2.3 %collective-permute-start.1 = (bf16[2064,128]{1,0:T(8,128)(2,1)S(1)}, bf16[2064,128]{1,0:T(8,128)(2,1)S(1)}, u32[]{:S(2)}, u32[]{:S(2)}) collective-permute-start(bf16[2064,128]{1,0:T(8,128)(2,1)S(1)} %get-tuple-element.13), channel_id=1, source_target_pairs={{0,1},{1,0},{2,3},{3,2},{4,5},{5,4},{6,7},{7,6},{8,9},{9,8},{10,11... | collective-permute-start | bytes 1585160 | tf_op jit(solution)/shard_map/ppermute | solution.py:235
  23.3 0.0 collective-permute-done.4.near_mine
  23.3 2.9 %collective-permute-start.5 = (bf16[1040,128]{1,0:T(8,128)(2,1)S(1)}, bf16[1040,128]{1,0:T(8,128)(2,1)S(1)}, u32[]{:S(2)}, u32[]{:S(2)}) collective-permute-start(bf16[1040,128]{1,0:T(8,128)(2,1)S(1)} %collective-permute-done.4.near_mine), channel_id=1, source_target_pairs={{0,1},{1,0},{2,3},{3,2},{4,5},{5,4},{6,7},{7,6},{8,9},{9,8},{10,11... | collective-permute-start | bytes 798728 | tf_op jit(solution)/shard_map/ppermute | solution.py:235
  26.2 2.4 %collective-permute-done.2.far_mine = bf16[1040,128]{1,0:T(8,128)(2,1)S(1)} collective-permute-done((bf16[1040,128]{1,0:T(8,128)(2,1)S(1)}, bf16[1040,128]{1,0:T(8,128)(2,1)S(1)}, u32[]{:S(2)}, u32[]{:S(2)}) %collective-permute-start.2) | collective-permute-done | bytes 266272 | tf_op jit(solution)/shard_map/ppermute | solution.py:254
  28.6 2.8 %collective-permute-start.3 = (bf16[1040,128]{1,0:T(8,128)(2,1)S(1)}, bf16[1040,128]{1,0:T(8,128)(2,1)S(1)}, u32[]{:S(2)}, u32[]{:S(2)}) collective-permute-start(bf16[1040,128]{1,0:T(8,128)(2,1)S(1)} %collective-permute-done.2.far_mine), channel_id=1, source_target_pairs={{0,1},{1,0},{2,3},{3,2},{4,5},{5,4},{6,7},{7,6},{8,9},{9,8},{10,11... | collective-permute-start | bytes 798728 | tf_op jit(solution)/shard_map/ppermute | solution.py:235
  31.4 0.0 collective-permute-done.1.q_sent
  31.4 0.0 collective-permute-done.5.near_sent
  31.4 2.5 %attend_near.1 = (bf16[128,2048]{1,0:T(8,128)(2,1)}, f32[2048,128]{1,0:T(8,128)S(1)}, f32[2048,128]{1,0:T(8,128)S(1)}, f32[2048,128]{1,0:T(8,128)S(1)}, f32[8,128]{1,0:T(8,128)S(1)}) custom-call(bf16[1024,128]{1,0:T(8,128)(2,1)S(1)} %get-tuple-element.12.q_mine, bf16[2064,128]{1,0:T(8,128)(2,1)S(1)} %collective-permute-done.1.q_sent, ...), custom_call_target="tpu_custom_call" | custom-call | flops 1 | bytes 1 | tf_op jit(solution)/shard_map/attend_near/pallas_call | solution.py:270
  34.0 0.0 collective-permute-done.3.far_sent
  34.0 0.2 attend_far.1
  (4 shorter events, 0.0 us)
Async XLA Ops:
  0.0 12.7 %copy-start.3 = (bf16[128,4096]{1,0:T(8,128)(2,1)S(1)}, bf16[128,4096]{1,0:T(8,128)(2,1)}, u32[]{:S(2)}) copy-start(bf16[128,4096]{1,0:T(8,128)(2,1)} %own.3) | copy-start | bytes 3145732
  0.0 12.7 %copy-start.4 = (s32[128]{0:T(128)S(1)}, s32[128]{0:T(128)}, u32[]{:S(2)}) copy-start(s32[128]{0:T(128)} %param.6) | copy-start | bytes 1540
  0.0 12.7 %copy-start.1 = (bf16[4096,256]{1,0:T(8,128)(2,1)S(1)}, bf16[4096,256]{1,0:T(8,128)(2,1)}, u32[]{:S(2)}) copy-start(bf16[4096,256]{1,0:T(8,128)(2,1)} %ks.1) | copy-start | bytes 6291460
  0.0 12.7 %copy-start.2 = (bf16[4096,256]{1,0:T(8,128)(2,1)S(1)}, bf16[4096,256]{1,0:T(8,128)(2,1)}, u32[]{:S(2)}) copy-start(bf16[4096,256]{1,0:T(8,128)(2,1)} %vs.1) | copy-start | bytes 6291460
  0.0 15.2 %collective-permute-start = (bf16[128,4096]{1,0:T(8,128)(2,1)}, bf16[128,4096]{1,0:T(8,128)(2,1)S(1)}, u32[]{:S(2)}, u32[]{:S(2)}) collective-permute-start(bf16[128,4096]{1,0:T(8,128)(2,1)} %own.3), channel_id=1, source_target_pairs={{0,1},{1,0},{2,3},{3,2},{4,5},{5,4},{6,7},{7,6},{8,9},{9,8},{10,11... | collective-permute-start | bytes 3145736 | tf_op jit(solution)/shard_map/ppermute | solution.py:235
  12.7 5.8 %copy-start = (bf16[4096,1024]{1,0:T(8,128)(2,1)S(1)}, bf16[4096,1024]{1,0:T(8,128)(2,1)}, u32[]{:S(2)}) copy-start(bf16[4096,1024]{1,0:T(8,128)(2,1)} %w_query.1) | copy-start | bytes 25165828
  15.9 7.4 %collective-permute-start.4 = (bf16[1040,128]{1,0:T(8,128)(2,1)S(1)}, bf16[1040,128]{1,0:T(8,128)(2,1)S(1)}, u32[]{:S(2)}, u32[]{:S(2)}) collective-permute-start(bf16[1040,128]{1,0:T(8,128)(2,1)S(1)} %other_kv.1.pay), channel_id=1, source_target_pairs={{0,2},{2,4},{4,6},{6,8},{8,10},{10,12},{12,14},{14,16},{16,18},{18... | collective-permute-start | bytes 798728 | tf_op jit(solution)/shard_map/ppermute | solution.py:253
  17.2 11.4 %collective-permute-start.2 = (bf16[1040,128]{1,0:T(8,128)(2,1)S(1)}, bf16[1040,128]{1,0:T(8,128)(2,1)S(1)}, u32[]{:S(2)}, u32[]{:S(2)}) collective-permute-start(bf16[1040,128]{1,0:T(8,128)(2,1)S(1)} %other_kv.1.pay), channel_id=1, source_target_pairs={{0,4},{2,6},{4,8},{6,10},{8,12},{10,14},{12,16},{14,18},{16,20},{1... | collective-permute-start | bytes 798728 | tf_op jit(solution)/shard_map/ppermute | solution.py:254
  21.0 10.4 %collective-permute-start.1 = (bf16[2064,128]{1,0:T(8,128)(2,1)S(1)}, bf16[2064,128]{1,0:T(8,128)(2,1)S(1)}, u32[]{:S(2)}, u32[]{:S(2)}) collective-permute-start(bf16[2064,128]{1,0:T(8,128)(2,1)S(1)} %get-tuple-element.13), channel_id=1, source_target_pairs={{0,1},{1,0},{2,3},{3,2},{4,5},{5,4},{6,7},{7,6},{8,9},{9,8},{10,11... | collective-permute-start | bytes 1585160 | tf_op jit(solution)/shard_map/ppermute | solution.py:235
  23.3 8.1 %collective-permute-start.5 = (bf16[1040,128]{1,0:T(8,128)(2,1)S(1)}, bf16[1040,128]{1,0:T(8,128)(2,1)S(1)}, u32[]{:S(2)}, u32[]{:S(2)}) collective-permute-start(bf16[1040,128]{1,0:T(8,128)(2,1)S(1)} %collective-permute-done.4.near_mine), channel_id=1, source_target_pairs={{0,1},{1,0},{2,3},{3,2},{4,5},{5,4},{6,7},{7,6},{8,9},{9,8},{10,11... | collective-permute-start | bytes 798728 | tf_op jit(solution)/shard_map/ppermute | solution.py:235
  28.6 5.4 %collective-permute-start.3 = (bf16[1040,128]{1,0:T(8,128)(2,1)S(1)}, bf16[1040,128]{1,0:T(8,128)(2,1)S(1)}, u32[]{:S(2)}, u32[]{:S(2)}) collective-permute-start(bf16[1040,128]{1,0:T(8,128)(2,1)S(1)} %collective-permute-done.2.far_mine), channel_id=1, source_target_pairs={{0,1},{1,0},{2,3},{3,2},{4,5},{5,4},{6,7},{7,6},{8,9},{9,8},{10,11... | collective-permute-start | bytes 798728 | tf_op jit(solution)/shard_map/ppermute | solution.py:235
